TPU v7x, 128 devices: a whole 4x4x4 slice. The times are simulated.
128 devices in a mesh: seq: 32 (over z, x_hi, y), head: 4 (over x_lo, core).
Axes of the slice: x: 4 (x_hi: 2, x_lo: 2; x = x_hi * 2 + x_lo), y: 4, z: 4, core: 2. Of those that a mesh axis runs over, the one named last changes fastest.
Arguments:
- queries: bfloat16 [32768, 2048], P('seq', 'head'), may hold values from -4.5 to 4.5
- keys: bfloat16 [32768, 2048], P('seq', 'head'), may hold values from -4.5 to 4.5
- values: bfloat16 [32768, 2048], P('seq', 'head'), may hold values from -6 to 6
- out_grad: bfloat16 [32768, 2048], P('seq', 'head'), may hold values from -6 to 6
Outputs:
- query_grad: bfloat16 [32768, 2048], P(('seq', 'head'))
- key_grad: bfloat16 [32768, 2048], P(('seq', 'head'))
- value_grad: bfloat16 [32768, 2048], P(('seq', 'head'))
- summary_key_grad: float32 [512, 2048], P('seq', 'head')
- summary_value_grad: float32 [512, 2048], P('seq', 'head')
All inputs are finite; a program needn't handle non-finite values.
Results may differ from a plain program's by a relative error of at most 0.006.
Values may be sent and summed in bfloat16 or wider, within the bound.
A program may use at most 128 MiB of HBM per device.

v0:
```python
import jax
import jax.numpy as jnp
from jax import lax
from jax.sharding import PartitionSpec as P

HEAD_DIM = 128
SPAN = 64


def span_means(rows_array):
    count, cols = rows_array.shape
    grouped = rows_array.reshape(count // SPAN, SPAN, cols)
    return (jnp.sum(grouped, axis=1, dtype=jnp.float32) / SPAN).astype(jnp.bfloat16)


def attend_rows(queries, keys, values, out_grad, span_ids, summ_k, summ_v, grad_k, grad_v):
    count, cols = queries.shape
    heads = cols // HEAD_DIM
    scale = HEAD_DIM ** (-0.5)
    full = lax.Precision.HIGHEST
    total = summ_k.shape[0]
    scols = min(256, total)
    qrows = min(512, count)
    tile = 2 * SPAN
    ntile = qrows // tile
    lane = jnp.arange(tile, dtype=jnp.int32)
    local_mask = (lane[:, None] // SPAN == lane[None, :] // SPAN) & (lane[:, None] >= lane[None, :])
    summ_k_wide = summ_k.astype(jnp.float32)
    pieces_q, pieces_k, pieces_v = ([], [], [])

    def to_rows(local):
        return local.transpose(1, 0, 2).reshape(heads, qrows)

    def from_rows(stats):
        return stats.reshape(heads, ntile, tile).transpose(1, 0, 2)

    for block in range(count // qrows):
        low = block * qrows
        q_rows = queries[low : low + qrows].reshape(qrows, heads, HEAD_DIM)
        k_rows = keys[low : low + qrows].reshape(qrows, heads, HEAD_DIM)
        v_rows = values[low : low + qrows].reshape(qrows, heads, HEAD_DIM)
        d_rows = out_grad[low : low + qrows].reshape(qrows, heads, HEAD_DIM)
        q_wide = q_rows.astype(jnp.float32)
        d_wide = d_rows.astype(jnp.float32)
        q_tile = q_rows.reshape(ntile, tile, heads, HEAD_DIM)
        k_tile = k_rows.reshape(ntile, tile, heads, HEAD_DIM)
        v_tile = v_rows.reshape(ntile, tile, heads, HEAD_DIM)
        d_tile = d_rows.reshape(ntile, tile, heads, HEAD_DIM)
        row_span = jnp.repeat(span_ids[low // SPAN : (low + qrows) // SPAN], SPAN)
        trips = (jnp.max(row_span) + scols - 1) // scols
        local = (
            jnp.einsum("nqhe,nkhe->nhqk", q_tile, k_tile, preferred_element_type=jnp.float32)
            * scale
        )
        local = jnp.where(local_mask, local, -jnp.inf)
        dp_loc = jnp.einsum("nqhe,nkhe->nhqk", d_tile, v_tile, preferred_element_type=jnp.float32)
        top_loc = jnp.max(local, axis=-1)
        weights_loc = jnp.exp(local - top_loc[..., None])
        sum_loc = jnp.sum(weights_loc, axis=-1)
        dot_loc = jnp.sum(weights_loc * dp_loc, axis=-1)
        score_store = jnp.zeros((heads, qrows, total), jnp.float32)
        dprob_store = jnp.zeros((heads, qrows, total), jnp.float32)

        def first_pass(index, carry, q_rows=q_rows, d_rows=d_rows, row_span=row_span):
            top, mass, weighted, scores_all, dprobs_all = carry
            start = index * scols
            key_piece = lax.dynamic_slice_in_dim(summ_k, start, scols, 0).reshape(
                scols, heads, HEAD_DIM
            )
            val_piece = lax.dynamic_slice_in_dim(summ_v, start, scols, 0).reshape(
                scols, heads, HEAD_DIM
            )
            scores = (
                jnp.einsum("qhe,jhe->hqj", q_rows, key_piece, preferred_element_type=jnp.float32)
                * scale
            )
            seen = (start + jnp.arange(scols, dtype=jnp.int32))[None, :] < row_span[:, None]
            scores = jnp.where(seen[None], scores, -jnp.inf)
            dprobs = jnp.einsum(
                "qhe,jhe->hqj", d_rows, val_piece, preferred_element_type=jnp.float32
            )
            new_top = jnp.maximum(top, jnp.max(scores, axis=-1))
            factor = jnp.exp(top - new_top)
            expo = jnp.exp(scores - new_top[..., None])
            mass = mass * factor + jnp.sum(expo, axis=-1)
            weighted = weighted * factor + jnp.sum(expo * dprobs, axis=-1)
            scores_all = lax.dynamic_update_slice_in_dim(scores_all, scores, start, 2)
            dprobs_all = lax.dynamic_update_slice_in_dim(dprobs_all, dprobs, start, 2)
            return (new_top, mass, weighted, scores_all, dprobs_all)

        start_carry = (
            to_rows(top_loc),
            to_rows(sum_loc),
            to_rows(dot_loc),
            score_store,
            dprob_store,
        )
        top, mass, weighted, score_store, dprob_store = lax.fori_loop(
            0, trips, first_pass, start_carry
        )
        lse = top + jnp.log(mass)
        delta = weighted / mass
        p_loc = jnp.exp(local - from_rows(lse)[..., None])
        g_loc = (p_loc * (dp_loc - from_rows(delta)[..., None])).astype(jnp.bfloat16)
        pb_loc = p_loc.astype(jnp.bfloat16)
        dq_loc = jnp.einsum("nhqk,nkhe->nqhe", g_loc, k_tile, preferred_element_type=jnp.float32)
        dk_loc = (
            jnp.einsum("nhqk,nqhe->nkhe", g_loc, q_tile, preferred_element_type=jnp.float32) * scale
        )
        dv_loc = jnp.einsum("nhqk,nqhe->nkhe", pb_loc, d_tile, preferred_element_type=jnp.float32)

        def grad_pass(
            index,
            carry,
            lse=lse,
            delta=delta,
            q_wide=q_wide,
            d_wide=d_wide,
            score_store=score_store,
            dprob_store=dprob_store,
        ):
            dq_acc, acc_k, acc_v = carry
            start = index * scols
            key_piece = lax.dynamic_slice_in_dim(summ_k_wide, start, scols, 0).reshape(
                scols, heads, HEAD_DIM
            )
            scores = lax.dynamic_slice_in_dim(score_store, start, scols, 2)
            dprobs = lax.dynamic_slice_in_dim(dprob_store, start, scols, 2)
            probs = jnp.exp(scores - lse[..., None])
            g_sum = probs * (dprobs - delta[..., None])
            dq_acc = dq_acc + jnp.einsum("hqj,jhe->qhe", g_sum, key_piece, precision=full)
            part_k = (
                jnp.einsum("hqj,qhe->jhe", g_sum, q_wide, precision=full).reshape(scols, cols)
                * scale
            )
            part_v = jnp.einsum("hqj,qhe->jhe", probs, d_wide, precision=full).reshape(scols, cols)
            acc_k = lax.dynamic_update_slice_in_dim(
                acc_k, lax.dynamic_slice_in_dim(acc_k, start, scols, 0) + part_k, start, 0
            )
            acc_v = lax.dynamic_update_slice_in_dim(
                acc_v, lax.dynamic_slice_in_dim(acc_v, start, scols, 0) + part_v, start, 0
            )
            return (dq_acc, acc_k, acc_v)

        dq_start = dq_loc.reshape(qrows, heads, HEAD_DIM)
        dq_sum, grad_k, grad_v = lax.fori_loop(0, trips, grad_pass, (dq_start, grad_k, grad_v))
        pieces_q.append((dq_sum * scale).reshape(qrows, cols))
        pieces_k.append(dk_loc.reshape(qrows, cols))
        pieces_v.append(dv_loc.reshape(qrows, cols))
    joined_q = jnp.concatenate(pieces_q, axis=0)
    joined_k = jnp.concatenate(pieces_k, axis=0)
    joined_v = jnp.concatenate(pieces_v, axis=0)
    return (joined_q, joined_k, joined_v, grad_k, grad_v)


def per_device(queries, keys, values, out_grad):
    count, cols = queries.shape
    per_dev = count // SPAN
    here = lax.axis_index("seq")
    nseq = lax.axis_size("seq")
    total = per_dev * nseq
    summ_k, summ_v = (
        lax.all_gather(span_means(keys), "seq", axis=0, tiled=True),
        lax.all_gather(span_means(values), "seq", axis=0, tiled=True),
    )
    zeros = jnp.zeros((total, cols), jnp.float32)
    own_ids = here * per_dev + jnp.arange(per_dev, dtype=jnp.int32)
    dq_rows, dk_rows, dv_rows, grad_k, grad_v = attend_rows(
        queries, keys, values, out_grad, own_ids, summ_k, summ_v, zeros, zeros
    )
    grad_k, grad_v = (
        lax.psum_scatter(grad_k, "seq", scatter_dimension=0, tiled=True),
        lax.psum_scatter(grad_v, "seq", scatter_dimension=0, tiled=True),
    )
    key_grad = (dk_rows + jnp.repeat(grad_k, SPAN, axis=0) / SPAN).astype(jnp.bfloat16)
    value_grad = (dv_rows + jnp.repeat(grad_v, SPAN, axis=0) / SPAN).astype(jnp.bfloat16)
    query_grad = dq_rows.astype(jnp.bfloat16)
    query_grad, key_grad, value_grad = (
        lax.all_to_all(query_grad, "head", split_axis=0, concat_axis=1, tiled=True),
        lax.all_to_all(key_grad, "head", split_axis=0, concat_axis=1, tiled=True),
        lax.all_to_all(value_grad, "head", split_axis=0, concat_axis=1, tiled=True),
    )
    return (query_grad, key_grad, value_grad, grad_k, grad_v)


def solution(mesh):
    placed = (P("seq", "head"), P("seq", "head"), P("seq", "head"), P("seq", "head"))
    return jax.shard_map(
        per_device,
        mesh=mesh,
        in_specs=placed,
        out_specs=(
            P(("seq", "head"), None),
            P(("seq", "head"), None),
            P(("seq", "head"), None),
            P("seq", "head"),
            P("seq", "head"),
        ),
        check_vma=False,
    )
```

profile of v0, /device:TPU:1, one launch (start us, length us, event | category | flops | bytes accessed | tf_op | source)
XLA Modules:
  0.0 768.6 jit_solution(12173668042832429576)
XLA Ops:
  8.7 2.2 fusion.39
  13.1 85.6 %all_gather.6 = bf16[512,512]{1,0:T(8,128)(2,1)S(1)} all-gather(bf16[16,512]{1,0:T(8,128)(2,1)S(1)} %multiply_convert_fusion.5), channel_id=1, replica_groups=mesh['seq'=32,'head'=4] {'seq'}, dimensions={0}, use_global_device_ids=true | all-gather | bytes 540672 | tf_op jit(solution)/shard_map/all_gather | solution.py:163
  113.5 2.2 copy.249
  115.7 2.0 reshape_reshape.29
  119.1 2.1 reshape_reshape.31
  121.3 81.3 %all_gather.7 = bf16[512,512]{1,0:T(8,128)(2,1)} all-gather(bf16[16,512]{1,0:T(8,128)(2,1)S(1)} %multiply_convert_fusion.4), channel_id=1, replica_groups=mesh['seq'=32,'head'=4] {'seq'}, dimensions={0}, use_global_device_ids=true | all-gather | bytes 540672 | tf_op jit(solution)/shard_map/all_gather | solution.py:164
  202.6 2.1 copy.235
  204.6 1.7 fusion.45
  208.8 2.5 broadcast.186.clone
  211.4 2.5 broadcast.186.clone.1
  213.8 5.7 while.69
  215.1 1.6 fusion.114
  216.8 2.7 fusion.115
  219.6 1.8 multiply_convert_fusion.1
  222.9 2.6 copy.264
  228.9 2.1 reshape_reshape.27
  231.1 2.5 fusion.44
  233.6 2.9 multiply_reduce_fusion.1
  236.4 2.5 broadcast.186.clone.2
  238.9 2.5 broadcast.186.clone.3
  241.5 4.6 while.68
  243.4 2.7 fusion.109
  246.1 1.8 multiply_convert_fusion.3
  252.3 20.7 %while.66 = (s32[]{:T(128)}, f32[512,4,128]{0,2,1:T(8,128)}, f32[512,512]{0,1:T(8,128)}, f32[512,512]{0,1:T(8,128)}, s32[]{:T(128)}, /*index=5*/f32[512,512]{0,1...) while((s32[]{:T(128)}, f32[512,4,128]{0,2,1:T(8,128)}, ...), condition=%wide.region_12.13_spmd, body=%wide.region_11.12_spmd.sunk | while | flops 2420244480 | bytes 79208928 | solution.py:146
  253.4 1.8 constant_dynamic-slice_fusion.19
  255.1 1.8 copy.353
  257.0 3.1 constant_dynamic-slice_fusion.20
  260.1 1.9 copy.354
  262.0 5.5 fusion.97
  267.5 1.8 fusion.98
  269.3 2.1 convolution_multiply_fusion.8
  273.1 20.7 %while.67 = (s32[]{:T(128)}, f32[512,4,128]{0,2,1:T(8,128)}, f32[512,512]{0,1:T(8,128)}, f32[512,512]{0,1:T(8,128)}, s32[]{:T(128)}, /*index=5*/f32[512,512]{0,1...) while((s32[]{:T(128)}, f32[512,4,128]{0,2,1:T(8,128)}, ...), condition=%wide.region_23.24_spmd, body=%wide.region_22.23_spmd.sunk | while | flops 2420244480 | bytes 79208928 | solution.py:146
  274.1 1.8 constant_dynamic-slice_fusion.22
  275.9 1.8 copy.355
  277.7 3.1 constant_dynamic-slice_fusion.23
  280.8 1.9 copy.356
  282.7 5.4 fusion.102
  288.2 1.8 fusion.103
  290.0 2.1 convolution_multiply_fusion.9
  293.8 2.6 copy.276
  300.4 32.1 %all-to-all-start = ((bf16[4,256,512]{2,1,0:T(8,128)(2,1)}), bf16[4,256,512]{2,1,0:T(8,128)(2,1)S(1)}, u32[]{:S(2)}, u32[]{:S(2)}) async-start(bf16[4,256,512]{2,1,0:T(8,128)(2,1)} %bitcast.240), calls=%async_computation | async-start | bytes 2097152 | tf_op jit(solution)/shard_map/all_to_all | solution.py:179
  332.6 2.6 fusion.16
  339.0 2.3 copy.347
  343.1 188.5 %reduce-scatter.3.cloned.1.call-done = f32[16,512]{1,0:T(8,128)} async-done(((f32[512,512]{1,0:T(8,128)}), f32[16,512]{1,0:T(8,128)}) %reduce-scatter.3.cloned.1.call-update) | async-done | bytes 32784 | tf_op jit(solution)/shard_map/reduce_scatter | solution.py:172
  533.9 30.1 %all-to-all-start.1 = ((bf16[4,256,512]{2,1,0:T(8,128)(2,1)}), bf16[4,256,512]{2,1,0:T(8,128)(2,1)}, u32[]{:S(2)}, u32[]{:S(2)}) async-start(bf16[4,256,512]{2,1,0:T(8,128)(2,1)} %fusion.15), calls=%async_computation.2 | async-start | bytes 2097152 | tf_op jit(solution)/shard_map/all_to_all | solution.py:180
  566.9 147.9 %reduce-scatter.5.cloned.1.call-done = f32[16,512]{1,0:T(8,128)} async-done(((f32[512,512]{1,0:T(8,128)}), f32[16,512]{1,0:T(8,128)}) %reduce-scatter.5.cloned.1.call-update) | async-done | bytes 32784 | tf_op jit(solution)/shard_map/reduce_scatter | solution.py:173
  717.2 29.1 %all-to-all-start.2 = ((bf16[4,256,512]{2,1,0:T(8,128)(2,1)}), bf16[4,256,512]{2,1,0:T(8,128)(2,1)S(1)}, u32[]{:S(2)}, u32[]{:S(2)}) async-start(bf16[4,256,512]{2,1,0:T(8,128)(2,1)} %fusion.14), calls=%async_computation.4 | async-start | bytes 2097152 | tf_op jit(solution)/shard_map/all_to_all | solution.py:181
  751.1 8.7 %all-to-all-done.2 = bf16[4,256,512]{2,1,0:T(8,128)(2,1)S(1)} async-done(((bf16[4,256,512]{2,1,0:T(8,128)(2,1)}), bf16[4,256,512]{2,1,0:T(8,128)(2,1)S(1)}, u32[]{:S(2)}, u32[]{:S(2)}) %all-to-all-start.2) | async-done | bytes 1048608 | tf_op jit(solution)/shard_map/all_to_all | solution.py:181
  (195 shorter events, 62.7 us)
Async XLA Ops:
  7.2 3.8 copy-start.33
  7.2 4.0 copy-start.34
  7.2 524.4 %reduce-scatter.3.cloned.1.call-start = ((), (), s32[]{:S(2)}) async-start(), calls=%async_computation.5 | async-start | bytes 1081344 | tf_op jit(solution)/shard_map/reduce_scatter | solution.py:172
  102.6 1.6 copy-start.46
  107.9 3.1 copy-start.45
  119.1 87.3 %copy-start.25 = (bf16[4,128,4,128]{3,1,2,0:T(8,128)(2,1)}, bf16[4,128,4,128]{3,1,2,0:T(8,128)(2,1)S(1)}, u32[]{:S(2)}) copy-start(bf16[4,128,4,128]{3,1,2,0:T(8,128)(2,1)S(1)} %copy.253) | copy-start | bytes 1572868
  204.6 2.7 copy-start.44
  219.5 1.9 copy-start.42
  221.4 1.4 copy-start.29
  221.8 3.7 copy-start.38
  222.9 3.7 copy-start.41
  226.6 4.5 copy-start.39
  228.9 7.5 copy-start.27
  238.9 2.6 copy-start.21
  246.1 1.9 copy-start.43
  252.3 1.0 copy-start.15
  262.0 5.5 copy-start.14
  267.5 1.8 copy-start
  267.5 1.9 copy-start.20
  269.3 2.1 copy-start.4
  269.3 2.1 copy-start.8
  271.4 1.6 copy-start.16
  271.7 1.3 copy-start.9
  273.1 1.0 copy-start.17
  282.7 5.5 copy-start.13
  288.2 1.8 copy-start.1
  288.2 1.9 copy-start.19
  290.0 2.1 copy-start.6
  290.0 2.1 copy-start.10
  292.1 1.6 copy-start.18
  292.4 1.3 copy-start.11
  293.8 2.7 copy-start.12
  296.4 1.4 copy-start.2
  296.4 418.4 %reduce-scatter.5.cloned.1.call-start = ((), (), s32[]{:S(2)}) async-start(), calls=%async_computation.6 | async-start | bytes 1081344 | tf_op jit(solution)/shard_map/reduce_scatter | solution.py:173
  297.8 1.2 copy-start.3
  299.4 33.2 %copy-start.30 = (bf16[4,4,128,128]{2,3,1,0:T(8,128)(2,1)S(1)}, bf16[4,4,128,128]{2,3,1,0:T(8,128)(2,1)}, u32[]{:S(2)}) copy-start(bf16[4,4,128,128]{2,3,1,0:T(8,128)(2,1)} %copy-done.29) | copy-start | bytes 1572868
  300.4 34.7 %copy-start.23 = (f32[4,4,128,128]{2,3,1,0:T(8,128)S(1)}, f32[4,4,128,128]{2,3,1,0:T(8,128)}, u32[]{:S(2)}) copy-start(f32[4,4,128,128]{2,3,1,0:T(8,128)} %copy-done.22) | copy-start | bytes 3145732
  300.4 34.7 %copy-start.26 = (bf16[4,128,4,128]{3,1,2,0:T(8,128)(2,1)S(1)}, bf16[4,128,4,128]{3,1,2,0:T(8,128)(2,1)}, u32[]{:S(2)}) copy-start(bf16[4,128,4,128]{3,1,2,0:T(8,128)(2,1)} %copy-done.25) | copy-start | bytes 1572868
  300.4 233.5 %all-to-all-start = ((bf16[4,256,512]{2,1,0:T(8,128)(2,1)}), bf16[4,256,512]{2,1,0:T(8,128)(2,1)S(1)}, u32[]{:S(2)}, u32[]{:S(2)}) async-start(bf16[4,256,512]{2,1,0:T(8,128)(2,1)} %bitcast.240), calls=%async_computation | async-start | bytes 2097152 | tf_op jit(solution)/shard_map/all_to_all | solution.py:179
  332.6 3.9 copy-start.32
  332.6 3.9 copy-start.40
  336.5 1.2 copy-start.36
  341.7 1.2 copy-start.37
  533.9 30.1 %copy-start.24 = (f32[4,4,128,128]{2,3,1,0:T(8,128)S(1)}, f32[4,4,128,128]{2,3,1,0:T(8,128)}, u32[]{:S(2)}) copy-start(f32[4,4,128,128]{2,3,1,0:T(8,128)} %get-tuple-element.711) | copy-start | bytes 3145732
  533.9 30.1 %copy-start.28 = (bf16[4,128,4,128]{3,1,2,0:T(8,128)(2,1)S(1)}, bf16[4,128,4,128]{3,1,2,0:T(8,128)(2,1)}, u32[]{:S(2)}) copy-start(bf16[4,128,4,128]{3,1,2,0:T(8,128)(2,1)} %copy-done.27) | copy-start | bytes 1572868
  533.9 183.2 %all-to-all-start.1 = ((bf16[4,256,512]{2,1,0:T(8,128)(2,1)}), bf16[4,256,512]{2,1,0:T(8,128)(2,1)}, u32[]{:S(2)}, u32[]{:S(2)}) async-start(bf16[4,256,512]{2,1,0:T(8,128)(2,1)} %fusion.15), calls=%async_computation.2 | async-start | bytes 2097152 | tf_op jit(solution)/shard_map/all_to_all | solution.py:180
  564.0 1.2 copy-start.35
  717.2 42.6 %all-to-all-start.2 = ((bf16[4,256,512]{2,1,0:T(8,128)(2,1)}), bf16[4,256,512]{2,1,0:T(8,128)(2,1)S(1)}, u32[]{:S(2)}, u32[]{:S(2)}) async-start(bf16[4,256,512]{2,1,0:T(8,128)(2,1)} %fusion.14), calls=%async_computation.4 | async-start | bytes 2097152 | tf_op jit(solution)/shard_map/all_to_all | solution.py:181
  (4 other events, 3.7 us)
Sparse Core Ops, SparseCore 0:
  296.6 234.9 reduce-scatter.2
  534.6 180.1 reduce-scatter.4
where the time goes:
time: 771 us; the launch traced here: 769 us
  waiting for transfers between devices  345 us (45%)
  blocking collectives  167 us (22%)
  local copies, waits for them, and re-layouts  92.7 us (12%)
  starting transfers between devices  91.3 us (12%)
  matrix products  40.2 us (5%)
  other arithmetic  16.1 us (2%)
  between operations  15.8 us (2%)
    reduce_scatter x1, waiting for transfers between devices, per_device(): lax.psum_scatter(grad_k, 'seq', scatter_dimension=0, tiled=True)  188 us
    reduce_scatter x1, waiting for transfers between devices, per_device(): lax.psum_scatter(grad_v, 'seq', scatter_dimension=0, tiled=True)  148 us
    all_gather x1, blocking collectives, per_device(): lax.all_gather(span_means(keys), 'seq', axis=0, tiled=True)  85.6 us
    all_gather x1, blocking collectives, per_device(): lax.all_gather(span_means(values), 'seq', axis=0, tiled=True)  81.3 us
    all_to_all x1, starting transfers between devices, per_device(): lax.all_to_all(query_grad, 'head', split_axis=0, concat_axis=1, tiled=True)  32.1 us
    all_to_all x1, starting transfers between devices, per_device(): lax.all_to_all(key_grad, 'head', split_axis=0, concat_axis=1, tiled=True)  30.1 us
    all_to_all x1, starting transfers between devices, per_device(): lax.all_to_all(value_grad, 'head', split_axis=0, concat_axis=1, tiled=True)  29.1 us
    unnamed x75, local copies, waits for them, and re-layouts  17.9 us
  transfers between devices with their start and end apart: 5, of which 3 were waited for; matrix products, arithmetic and copies ran while one was open for 3% of the time, Pallas kernels for 0%

commit v1 on v0

v1 whole, which is shorter than its diff:
```python
import functools

import jax
import jax.numpy as jnp
from jax import lax
from jax.experimental import pallas as pl
from jax.experimental.pallas import tpu as pltpu
from jax.sharding import PartitionSpec as P

HEAD_DIM = 128
SPAN = 64
MESH = pl.DeviceIdType.MESH
LOG2E = 1.4426950408889634
F32 = jnp.float32
BF16 = jnp.bfloat16
NT = (((1,), (1,)), ((), ()))
NN = (((1,), (0,)), ((), ()))
TN = (((0,), (0,)), ((), ()))


def dot(a, b, dims):
    return lax.dot_general(a, b, dims, preferred_element_type=F32)


def tile_order(hd, j):
    chip = lax.rem(hd // 2 + 1 + j // 2, 2)
    core = lax.rem(lax.rem(hd, 2) + j + j // 2, 2)
    return chip * 2 + core


def main_kernel(
    nseq,
    nhead,
    q_hbm, k_hbm, v_hbm, d_hbm,
    out, gk_out, gv_out, shared,
    q_ref, k_ref, v_ref, d_ref,
    summ, summ_t, acc, term, rterm, own, sgs, stage, s_scr, e_scr, dp_scr,
    load_sem, gsend, grecv, rsend, rrecv, asend, arecv, local_sem, ssend, srecv, own_sem,
):
    me = lax.axis_index("seq")
    hd = lax.axis_index("head")
    count = q_ref.shape[0]
    heads = q_ref.shape[1] // HEAD_DIM
    per_dev = count // SPAN
    total = per_dev * nseq
    tile = count // nhead
    scale = HEAD_DIM ** (-0.5)
    c2 = scale * LOG2E

    loads = [
        pltpu.make_async_copy(src, dst, load_sem.at[i])
        for i, (src, dst) in enumerate(
            ((k_hbm, k_ref), (v_hbm, v_ref), (q_hbm, q_ref), (d_hbm, d_ref))
        )
    ]
    for load in loads:
        load.start()
    summ[...] = jnp.zeros(summ.shape, summ.dtype)

    barrier = pltpu.get_barrier_semaphore()

    def greet(i, _):
        pl.semaphore_signal(
            barrier, inc=1, device_id={"seq": lax.rem(me + i, nseq)}, device_id_type=MESH
        )
        return 0

    lax.fori_loop(1, nseq, greet, 0)
    for i in range(1, nhead):
        pl.semaphore_signal(
            barrier, inc=1, device_id={"head": lax.rem(hd + i, nhead)}, device_id_type=MESH
        )

    pool = (
        lax.broadcasted_iota(jnp.int32, (per_dev, count), 1) // SPAN
        == lax.broadcasted_iota(jnp.int32, (per_dev, count), 0)
    ).astype(BF16)
    loads[0].wait()
    mean_k = (dot(pool, k_ref[...], NN) * (1.0 / SPAN)).astype(BF16)
    loads[1].wait()
    mean_v = (dot(pool, v_ref[...], NN) * (1.0 / SPAN)).astype(BF16)
    summ[me, 0] = mean_k
    summ[me, 1] = mean_v

    pl.semaphore_wait(barrier, nseq - 1 + nhead - 1)

    def gather_copy(src, dst):
        return pltpu.make_async_remote_copy(
            src_ref=summ.at[src],
            dst_ref=summ.at[src],
            send_sem=gsend.at[dst],
            recv_sem=grecv.at[src],
            device_id={"seq": dst},
            device_id_type=MESH,
        )

    def gather_start(dst, _):
        gather_copy(me, dst).start()
        return 0

    lax.fori_loop(me + 1, nseq, gather_start, 0)
    loads[2].wait()
    loads[3].wait()

    def gather_wait(src, _):
        gather_copy(src, 0).wait_recv()
        return 0

    lax.fori_loop(0, me, gather_wait, 0)

    rows = 128
    nchunk = total // rows
    shards = rows // per_dev
    lane = lax.broadcasted_iota(jnp.int32, (SPAN, tile), 1)
    low_lane = lax.rem(lane, 2 * SPAN) < SPAN
    causal = lax.broadcasted_iota(jnp.int32, (SPAN, tile), 0) <= lax.rem(lane, SPAN)
    low128 = low_lane[:, : 2 * SPAN]

    def fold(x, op):
        parts = [x[8 * i : 8 * i + 8] for i in range(x.shape[0] // 8)]
        while len(parts) > 1:
            parts = [
                op(parts[i], parts[i + 1]) if i + 1 < len(parts) else parts[i]
                for i in range(0, len(parts), 2)
            ]
        return parts[0]

    def step(n, _):
        h = n // nhead
        j = lax.rem(n, nhead)
        i = tile_order(hd, j)
        cols = pl.ds(pl.multiple_of(h * HEAD_DIM, HEAD_DIM), HEAD_DIM)
        trow = pl.ds(pl.multiple_of(i * tile, tile), tile)

        def sk(c):
            return summ[c * shards : (c + 1) * shards, 0, :, cols].reshape(rows, HEAD_DIM)

        def sv(c):
            return summ[c * shards : (c + 1) * shards, 1, :, cols].reshape(rows, HEAD_DIM)

        @pl.when(j == 0)
        def _():
            for c in range(nchunk):
                summ_t[:, c * rows : (c + 1) * rows] = sk(c).astype(F32).T.astype(BF16)
            acc[...] = jnp.zeros(acc.shape, F32)

        qt = q_ref[trow, cols]
        kt = k_ref[trow, cols]
        vt = v_ref[trow, cols]
        dt = d_ref[trow, cols]

        def local(a, b):
            picked = []
            for p in range(tile // (2 * SPAN)):
                sl = slice(p * 2 * SPAN, (p + 1) * 2 * SPAN)
                full = dot(a[sl], b[sl], NT)
                picked.append(jnp.where(low128, full[:SPAN], full[SPAN:]))
            return jnp.concatenate(picked, axis=1)

        a_loc = jnp.where(causal, local(kt, qt), -jnp.inf)
        dp_loc = local(vt, dt)
        span_of = (
            me * per_dev
            + i * (tile // SPAN)
            + lax.broadcasted_iota(jnp.int32, (rows, tile), 1) // SPAN
        )
        row_id = lax.broadcasted_iota(jnp.int32, (rows, tile), 0)
        top = fold(a_loc, jnp.maximum)
        for c in range(nchunk):
            s = dot(sk(c), qt, NT)
            s = jnp.where(row_id + c * rows < span_of, s, -jnp.inf)
            s_scr[c * rows : (c + 1) * rows] = s
            top = jnp.maximum(top, fold(s, jnp.maximum))
        top = jnp.max(top, axis=0, keepdims=True)
        base = top * c2

        e_loc = jnp.exp2(a_loc * c2 - base)
        mass = fold(e_loc, jnp.add)
        weighted = fold(e_loc * dp_loc, jnp.add)
        for c in range(nchunk):
            sl = slice(c * rows, (c + 1) * rows)
            dp = dot(sv(c), dt, NT)
            e = jnp.exp2(s_scr[sl] * c2 - base)
            e_scr[sl] = e
            dp_scr[sl] = dp
            mass = mass + fold(e, jnp.add)
            weighted = weighted + fold(e * dp, jnp.add)
        inv = 1.0 / jnp.sum(mass, axis=0, keepdims=True)
        delta = jnp.sum(weighted, axis=0, keepdims=True) * inv

        p_loc = e_loc * inv
        g_loc = p_loc * (dp_loc - delta)
        zero = jnp.zeros((SPAN, 2 * SPAN), F32)
        dqt_parts = []
        for p in range(tile // (2 * SPAN)):
            sl = slice(p * 2 * SPAN, (p + 1) * 2 * SPAN)
            g = g_loc[:, sl]
            w = p_loc[:, sl]
            g2 = jnp.concatenate(
                [jnp.where(low128, g, zero), jnp.where(low128, zero, g)], axis=0
            ).astype(BF16)
            w2 = jnp.concatenate(
                [jnp.where(low128, w, zero), jnp.where(low128, zero, w)], axis=0
            ).astype(BF16)
            stage[n, 1, sl] = (dot(g2, qt[sl], NN) * scale).astype(BF16)
            stage[n, 2, sl] = dot(w2, dt[sl], NN).astype(BF16)
            dqt_parts.append(dot(kt[sl], g2, TN))
        dqt = jnp.concatenate(dqt_parts, axis=1)
        for c in range(nchunk):
            sl = slice(c * rows, (c + 1) * rows)
            r = e_scr[sl] * inv
            g = (r * (dp_scr[sl] - delta)).astype(BF16)
            acc[0, sl] += dot(g, qt, NN)
            acc[1, sl] += dot(r.astype(BF16), dt, NN)
            dqt = dqt + dot(summ_t[:, sl], g, NN)
        stage[n, 0] = (dqt * scale).T.astype(BF16)

        slot = hd * heads + h

        @pl.when(j < nhead - 1)
        def _():
            pltpu.make_async_remote_copy(
                src_ref=stage.at[n],
                dst_ref=out.at[slot],
                send_sem=asend.at[n],
                recv_sem=arecv.at[hd],
                device_id={"head": i},
                device_id_type=MESH,
            ).start()

        @pl.when(j == nhead - 1)
        def _():
            pltpu.make_async_copy(stage.at[n], out.at[slot], local_sem.at[h]).start()
            for w in range(2):
                term[:, h, w] = acc[w].reshape(nseq, per_dev, HEAD_DIM).astype(BF16)
                own[w, :, cols] = acc[w, pl.ds(pl.multiple_of(me * per_dev, per_dev), per_dev)]

            def send_term(k, _):
                dst = me - 1 - k
                pltpu.make_async_remote_copy(
                    src_ref=term.at[dst, h],
                    dst_ref=rterm.at[me, h],
                    send_sem=rsend.at[dst],
                    recv_sem=rrecv.at[me],
                    device_id={"seq": dst},
                    device_id_type=MESH,
                ).start()
                return 0

            lax.fori_loop(0, me, send_term, 0)

        return 0

    lax.fori_loop(0, heads * nhead, step, 0)

    def term_all(a, b):
        return pltpu.make_async_remote_copy(
            src_ref=term.at[a],
            dst_ref=rterm.at[b],
            send_sem=rsend.at[a],
            recv_sem=rrecv.at[b],
            device_id={"seq": a},
            device_id_type=MESH,
        )

    def add_term(src, _):
        term_all(0, src).wait_recv()
        for w in range(2):
            for h in range(heads):
                sl = slice(h * HEAD_DIM, (h + 1) * HEAD_DIM)
                own[w, :, sl] += rterm[src, h, w].astype(F32)
        return 0

    lax.fori_loop(me + 1, nseq, add_term, 0)
    grad_k = own[0] * scale
    grad_v = own[1]
    gk_out[...] = grad_k
    gv_out[...] = grad_v
    part = per_dev // nhead
    for dst in range(nhead):
        sgs[dst, 0:part] = grad_k[dst * part : (dst + 1) * part] * (1.0 / SPAN)
        sgs[dst, part : 2 * part] = grad_v[dst * part : (dst + 1) * part] * (1.0 / SPAN)

    def shared_copy(src, dst, slot):
        return pltpu.make_async_remote_copy(
            src_ref=sgs.at[dst],
            dst_ref=shared.at[src],
            send_sem=ssend.at[slot],
            recv_sem=srecv.at[src],
            device_id={"head": dst},
            device_id_type=MESH,
        )

    for k in range(1, nhead):
        shared_copy(hd, lax.rem(hd + k, nhead), k).start()
    mine = pltpu.make_async_copy(sgs.at[hd], shared.at[hd], own_sem)
    mine.start()
    mine.wait()
    for k in range(1, nhead):
        other = lax.rem(hd + k, nhead)
        shared_copy(hd, other, k).wait_send()
        shared_copy(other, other, k).wait_recv()
        pltpu.make_async_remote_copy(
            src_ref=stage.at[0],
            dst_ref=out.at[pl.ds(other * heads, heads)],
            send_sem=asend.at[0],
            recv_sem=arecv.at[other],
            device_id={"head": other},
            device_id_type=MESH,
        ).wait_recv()

    def sent_all(n, _):
        @pl.when(lax.rem(n, nhead) < nhead - 1)
        def _():
            pltpu.make_async_remote_copy(
                src_ref=stage.at[n],
                dst_ref=out.at[0],
                send_sem=asend.at[n],
                recv_sem=arecv.at[hd],
                device_id={"head": lax.rem(hd + 1, nhead)},
                device_id_type=MESH,
            ).wait_send()

        return 0

    lax.fori_loop(0, heads * nhead, sent_all, 0)
    for h in range(heads):
        pltpu.make_async_copy(
            stage.at[h * nhead + nhead - 1], out.at[hd * heads + h], local_sem.at[h]
        ).wait()

    def gather_sent(dst, _):
        gather_copy(me, dst).wait_send()
        return 0

    lax.fori_loop(me + 1, nseq, gather_sent, 0)

    def terms_sent(dst, _):
        term_all(dst, me).wait_send()
        return 0

    lax.fori_loop(0, me, terms_sent, 0)


def finish_kernel(part, in_ref, shared_ref, q_out, k_out, v_out):
    heads = in_ref.shape[0]
    for h in range(heads):
        sl = slice(h * HEAD_DIM, (h + 1) * HEAD_DIM)
        q_out[:, sl] = in_ref[h, 0]
        for w, ref in ((0, k_out), (1, v_out)):
            for c in range(part):
                rows = slice(c * SPAN, (c + 1) * SPAN)
                add = shared_ref[0, w * part + c : w * part + c + 1, sl]
                ref[rows, sl] = (in_ref[h, 1 + w, rows].astype(F32) + add).astype(BF16)


def per_device(queries, keys, values, out_grad):
    count, cols = queries.shape
    nseq = lax.axis_size("seq")
    nhead = lax.axis_size("head")
    heads = cols // HEAD_DIM
    per_dev = count // SPAN
    total = per_dev * nseq
    tile = count // nhead
    part = per_dev // nhead
    steps = heads * nhead
    anyspace = pl.BlockSpec(memory_space=pl.ANY)
    vmem = pl.BlockSpec(memory_space=pltpu.VMEM)
    dma = pltpu.SemaphoreType.DMA
    pieces, grad_k, grad_v, shared = pl.pallas_call(
        functools.partial(main_kernel, nseq, nhead),
        out_shape=(
            jax.ShapeDtypeStruct((nhead * heads, 3, tile, HEAD_DIM), BF16),
            jax.ShapeDtypeStruct((per_dev, cols), F32),
            jax.ShapeDtypeStruct((per_dev, cols), F32),
            jax.ShapeDtypeStruct((nhead, 2 * part, cols), F32),
        ),
        in_specs=[anyspace] * 4,
        out_specs=(anyspace, vmem, vmem, anyspace),
        scratch_shapes=[pltpu.VMEM((count, cols), BF16)] * 4
        + [
            pltpu.VMEM((nseq, 2, per_dev, cols), BF16),
            pltpu.VMEM((HEAD_DIM, total), BF16),
            pltpu.VMEM((2, total, HEAD_DIM), F32),
            pltpu.VMEM((nseq, heads, 2, per_dev, HEAD_DIM), BF16),
            pltpu.VMEM((nseq, heads, 2, per_dev, HEAD_DIM), BF16),
            pltpu.VMEM((2, per_dev, cols), F32),
            pltpu.VMEM((nhead, 2 * part, cols), F32),
            pltpu.VMEM((steps, 3, tile, HEAD_DIM), BF16),
            pltpu.VMEM((total, tile), F32),
            pltpu.VMEM((total, tile), F32),
            pltpu.VMEM((total, tile), F32),
            dma((4,)),
            dma((nseq,)),
            dma((nseq,)),
            dma((nseq,)),
            dma((nseq,)),
            dma((steps,)),
            dma((nhead,)),
            dma((heads,)),
            dma((nhead,)),
            dma((nhead,)),
            dma,
        ],
        compiler_params=pltpu.CompilerParams(
            collective_id=0, has_side_effects=True, vmem_limit_bytes=40 * 1024 * 1024
        ),
        name="attend",
    )(queries, keys, values, out_grad)
    row = jax.ShapeDtypeStruct((tile, nhead * cols), BF16)
    col_block = pl.BlockSpec((tile, cols), lambda g: (0, g))
    query_grad, key_grad, value_grad = pl.pallas_call(
        functools.partial(finish_kernel, part),
        out_shape=(row, row, row),
        grid=(nhead,),
        in_specs=[
            pl.BlockSpec((heads, 3, tile, HEAD_DIM), lambda g: (g, 0, 0, 0)),
            pl.BlockSpec((1, 2 * part, cols), lambda g: (g, 0, 0)),
        ],
        out_specs=(col_block, col_block, col_block),
        name="finish",
    )(pieces, shared)
    return (query_grad, key_grad, value_grad, grad_k, grad_v)


def solution(mesh):
    placed = (P("seq", "head"), P("seq", "head"), P("seq", "head"), P("seq", "head"))
    return jax.shard_map(
        per_device,
        mesh=mesh,
        in_specs=placed,
        out_specs=(
            P(("seq", "head"), None),
            P(("seq", "head"), None),
            P(("seq", "head"), None),
            P("seq", "head"),
            P("seq", "head"),
        ),
        check_vma=False,
    )
```

time: 771 us -> 94.5 us (0.12)
  waiting for transfers between devices: 345 us -> 0 us
  blocking collectives: 167 us -> 0 us
  starting transfers between devices: 91.3 us -> 0 us
  Pallas kernels: 0 us -> 85.1 us
  local copies, waits for them, and re-layouts: 92.7 us -> 8.37 us
  matrix products: 40.2 us -> 0 us
  other arithmetic: 16.1 us -> 0 us
  between operations: 15.8 us -> 0.66 us
    reduce_scatter x2 -> x0, waiting for transfers between devices: 336 us -> none  [the longest x1 188 us: per_device(): lax.psum_scatter(grad_k, 'seq', scatter_dimension=0, tiled=True)]
    all_gather x2 -> x0, blocking collectives: 167 us -> none  [the longest x1 85.6 us: per_device(): lax.all_gather(span_means(keys), 'seq', axis=0, tiled=True)]
    all_to_all x3 -> x0, starting transfers between devices: 91.2 us -> none  [the longest x1 32.1 us: per_device(): lax.all_to_all(query_grad, 'head', split_axis=0, concat_axis=1, tiled=True)]
    pallas_call x0 -> x2, Pallas kernels: none -> 85.1 us  [the longest x1 80.9 us: per_device(): pl.pallas_call(functools.partial(main_kernel, nseq, nhead), out_shape=(ja...]
    dot_general x20 -> x0, matrix products: 40.2 us -> none  [the longest x2 10.9 us: grad_pass(): jnp.einsum('hqj,jhe->qhe', g_sum, key_piece, precision=full)]
    another operation x16 -> x0, local copies, waits for them, and re-layouts: 27 us -> none
    dynamic_slice x12 -> x0, local copies, waits for them, and re-layouts: 19.2 us -> none  [the longest x4 9.98 us: grad_pass(): scores = lax.dynamic_slice_in_dim(score_store, start, scols, 2)]
    while x43 -> x0, local copies, waits for them, and re-layouts: 12.9 us -> none  [the longest x5 8.08 us: attend_rows(): lax.fori_loop(0, trips, grad_pass, (dq_start, grad_k, grad_v))]
  transfers between devices with their start and end apart: 5 -> 0, of which waited for: 3 -> 0; matrix products, arithmetic and copies ran while one was open for 3% -> 0% of each run, Pallas kernels for 0% -> 0%
where the time goes in v1:
time: 94.5 us; the launch traced here: 94.2 us
  Pallas kernels  85.1 us (90%)
  local copies, waits for them, and re-layouts  8.37 us (9%)
    pallas_call x1, Pallas kernels, per_device(): pl.pallas_call(functools.partial(main_kernel, nseq, nhead), out_shape=(ja...  80.9 us
    unnamed x14, local copies, waits for them, and re-layouts  8.37 us
    pallas_call x1, Pallas kernels, per_device(): pl.pallas_call(functools.partial(finish_kernel, part), out_shape=(row, ro...  4.24 us

profile of v1, /device:TPU:1, one launch (start us, length us, event | category | flops | bytes accessed | tf_op | source)
XLA Modules:
  0.0 94.2 jit_solution(9938608274992987293)
XLA Ops:
  0.6 0.0 copy-start.1
  0.6 1.2 %copy-done.1 = bf16[1024,512]{1,0:T(8,128)(2,1)S(1)} copy-done((bf16[1024,512]{1,0:T(8,128)(2,1)S(1)}, bf16[1024,512]{1,0:T(8,128)(2,1)}, u32[]{:S(2)}) %copy-start.1) | copy-done | bytes 1048600
  1.9 0.0 copy-start.2
  1.9 1.2 %copy-done.2 = bf16[1024,512]{1,0:T(8,128)(2,1)S(1)} copy-done((bf16[1024,512]{1,0:T(8,128)(2,1)S(1)}, bf16[1024,512]{1,0:T(8,128)(2,1)}, u32[]{:S(2)}) %copy-start.2) | copy-done | bytes 1048600
  3.1 0.0 copy-start.3
  3.1 1.2 %copy-done.3 = bf16[1024,512]{1,0:T(8,128)(2,1)S(1)} copy-done((bf16[1024,512]{1,0:T(8,128)(2,1)S(1)}, bf16[1024,512]{1,0:T(8,128)(2,1)}, u32[]{:S(2)}) %copy-start.3) | copy-done | bytes 1048600
  4.3 0.0 copy-start.4
  4.3 1.2 %copy-done.4 = bf16[1024,512]{1,0:T(8,128)(2,1)S(1)} copy-done((bf16[1024,512]{1,0:T(8,128)(2,1)S(1)}, bf16[1024,512]{1,0:T(8,128)(2,1)}, u32[]{:S(2)}) %copy-start.4) | copy-done | bytes 1048600
  5.5 80.9 %attend.1 = (bf16[16,3,256,128]{3,2,1,0:T(8,128)(2,1)S(1)}, f32[16,512]{1,0:T(8,128)S(1)}, f32[16,512]{1,0:T(8,128)S(1)}, f32[4,8,512]{2,1,0:T(8,128)S(1)}) custom-call(bf16[1024,512]{1,0:T(8,128)(2,1)S(1)} %copy-done.1, bf16[1024,512]{1,0:T(8,128)(2,1)S(1)} %copy-done.2, bf16[1024,512]{1,0:T(8,128)(2,1)S(1)} %copy-done.3, bf16[1024,512]{1,0:T(8,128)(2,1)S(1)} %copy-done.4), custom_call_target="tpu_custom_call" | custom-call | tf_op jit(solution)/shard_map/attend/pallas_call | solution.py:370
  86.4 0.0 copy-start
  86.4 1.6 %copy-done = bf16[16,3,256,128]{3,2,1,0:T(8,128)(2,1)} copy-done((bf16[16,3,256,128]{3,2,1,0:T(8,128)(2,1)}, bf16[16,3,256,128]{3,2,1,0:T(8,128)(2,1)S(1)}, u32[]{:S(2)}) %copy-start) | copy-done | bytes 3145752
  88.1 0.0 copy-start.5
  88.1 0.6 copy-done.5
  88.7 4.2 %finish.1 = (bf16[256,2048]{1,0:T(8,128)(2,1)}, bf16[256,2048]{1,0:T(8,128)(2,1)}, bf16[256,2048]{1,0:T(8,128)(2,1)}) custom-call(bf16[16,3,256,128]{3,2,1,0:T(8,128)(2,1)} %copy-done, f32[4,8,512]{2,1,0:T(8,128)} %copy-done.5), custom_call_target="tpu_custom_call" | custom-call | tf_op jit(solution)/shard_map/finish/pallas_call | solution.py:412
  92.9 0.6 copy.11
  93.5 0.6 copy.12
Async XLA Ops:
  0.6 1.2 %copy-start.1 = (bf16[1024,512]{1,0:T(8,128)(2,1)S(1)}, bf16[1024,512]{1,0:T(8,128)(2,1)}, u32[]{:S(2)}) copy-start(bf16[1024,512]{1,0:T(8,128)(2,1)} %q_hbm.1) | copy-start | bytes 3145732
  1.9 1.2 %copy-start.2 = (bf16[1024,512]{1,0:T(8,128)(2,1)S(1)}, bf16[1024,512]{1,0:T(8,128)(2,1)}, u32[]{:S(2)}) copy-start(bf16[1024,512]{1,0:T(8,128)(2,1)} %k_hbm.1) | copy-start | bytes 3145732
  3.1 1.2 %copy-start.3 = (bf16[1024,512]{1,0:T(8,128)(2,1)S(1)}, bf16[1024,512]{1,0:T(8,128)(2,1)}, u32[]{:S(2)}) copy-start(bf16[1024,512]{1,0:T(8,128)(2,1)} %v_hbm.1) | copy-start | bytes 3145732
  4.3 1.2 %copy-start.4 = (bf16[1024,512]{1,0:T(8,128)(2,1)S(1)}, bf16[1024,512]{1,0:T(8,128)(2,1)}, u32[]{:S(2)}) copy-start(bf16[1024,512]{1,0:T(8,128)(2,1)} %d_hbm.1) | copy-start | bytes 3145732
  86.4 1.6 %copy-start = (bf16[16,3,256,128]{3,2,1,0:T(8,128)(2,1)}, bf16[16,3,256,128]{3,2,1,0:T(8,128)(2,1)S(1)}, u32[]{:S(2)}) copy-start(bf16[16,3,256,128]{3,2,1,0:T(8,128)(2,1)S(1)} %get-tuple-element.12.in_ref) | copy-start | bytes 9437188
  88.1 0.6 copy-start.5

commit v2 on v1

--- a/solution.py
+++ b/solution.py
@@ -9,6 +9,8 @@
 
 HEAD_DIM = 128
 SPAN = 64
+PLACES = 4
+SLAB = 8
 MESH = pl.DeviceIdType.MESH
 LOG2E = 1.4426950408889634
 F32 = jnp.float32
@@ -34,8 +36,9 @@
     q_hbm, k_hbm, v_hbm, d_hbm,
     out, gk_out, gv_out, shared,
     q_ref, k_ref, v_ref, d_ref,
-    summ, summ_t, acc, term, rterm, own, sgs, stage, s_scr, e_scr, dp_scr,
-    load_sem, gsend, grecv, rsend, rrecv, asend, arecv, local_sem, ssend, srecv, own_sem,
+    summ, summ_t, acc, term, rterm, own, other_own, sgs, stage, s_scr, e_scr, dp_scr,
+    load_sem, xsend, xrecv, gsend, grecv, rsend, rrecv, psend, precv,
+    asend, arecv, local_sem, ssend, srecv, own_sem,
 ):
     me = lax.axis_index("seq")
     hd = lax.axis_index("head")
@@ -46,26 +49,44 @@
     tile = count // nhead
     scale = HEAD_DIM ** (-0.5)
     c2 = scale * LOG2E
+    slab = me // SLAB
+    side = lax.rem(me, SLAB) // PLACES
+    plane = slab * PLACES + lax.rem(me, PLACES)
+    nplane = nseq // 2
+    partner = me + PLACES - 2 * PLACES * side
+
+    def shard_at(p):
+        return (p // PLACES) * SLAB + side * PLACES + lax.rem(p, PLACES)
 
     loads = [
-        pltpu.make_async_copy(src, dst, load_sem.at[i])
+        [
+            pltpu.make_async_copy(
+                src.at[c * tile : (c + 1) * tile], dst.at[c * tile : (c + 1) * tile], load_sem.at[i, c]
+            )
+            for c in range(nhead)
+        ]
         for i, (src, dst) in enumerate(
             ((k_hbm, k_ref), (v_hbm, v_ref), (q_hbm, q_ref), (d_hbm, d_ref))
         )
     ]
-    for load in loads:
-        load.start()
+    for group in loads:
+        for load in group:
+            load.start()
     summ[...] = jnp.zeros(summ.shape, summ.dtype)
 
     barrier = pltpu.get_barrier_semaphore()
 
     def greet(i, _):
         pl.semaphore_signal(
-            barrier, inc=1, device_id={"seq": lax.rem(me + i, nseq)}, device_id_type=MESH
+            barrier,
+            inc=1,
+            device_id={"seq": shard_at(lax.rem(plane + i, nplane))},
+            device_id_type=MESH,
         )
         return 0
 
-    lax.fori_loop(1, nseq, greet, 0)
+    lax.fori_loop(1, nplane, greet, 0)
+    pl.semaphore_signal(barrier, inc=1, device_id={"seq": partner}, device_id_type=MESH)
     for i in range(1, nhead):
         pl.semaphore_signal(
             barrier, inc=1, device_id={"head": lax.rem(hd + i, nhead)}, device_id_type=MESH
@@ -75,42 +96,62 @@
         lax.broadcasted_iota(jnp.int32, (per_dev, count), 1) // SPAN
         == lax.broadcasted_iota(jnp.int32, (per_dev, count), 0)
     ).astype(BF16)
-    loads[0].wait()
-    mean_k = (dot(pool, k_ref[...], NN) * (1.0 / SPAN)).astype(BF16)
-    loads[1].wait()
-    mean_v = (dot(pool, v_ref[...], NN) * (1.0 / SPAN)).astype(BF16)
-    summ[me, 0] = mean_k
-    summ[me, 1] = mean_v
-
-    pl.semaphore_wait(barrier, nseq - 1 + nhead - 1)
-
-    def gather_copy(src, dst):
+    for w, ref in ((0, k_ref), (1, v_ref)):
+        for load in loads[w]:
+            load.wait()
+        mean = (dot(pool, ref[...], NN) * (1.0 / SPAN)).astype(BF16)
+        for h in range(heads):
+            summ[h, plane, side, w] = mean[:, h * HEAD_DIM : (h + 1) * HEAD_DIM]
+
+    pl.semaphore_wait(barrier, nplane - 1 + 1 + nhead - 1)
+
+    def swap_copy(h, to):
         return pltpu.make_async_remote_copy(
-            src_ref=summ.at[src],
-            dst_ref=summ.at[src],
-            send_sem=gsend.at[dst],
-            recv_sem=grecv.at[src],
-            device_id={"seq": dst},
+            src_ref=summ.at[h, plane, to],
+            dst_ref=summ.at[h, plane, to],
+            send_sem=xsend.at[h],
+            recv_sem=xrecv.at[h],
+            device_id={"seq": partner},
             device_id_type=MESH,
         )
 
-    def gather_start(dst, _):
-        gather_copy(me, dst).start()
-        return 0
-
-    lax.fori_loop(me + 1, nseq, gather_start, 0)
-    loads[2].wait()
-    loads[3].wait()
-
-    def gather_wait(src, _):
-        gather_copy(src, 0).wait_recv()
-        return 0
-
-    lax.fori_loop(0, me, gather_wait, 0)
+    def gather_copy(h, src, dst):
+        return pltpu.make_async_remote_copy(
+            src_ref=summ.at[h, src],
+            dst_ref=summ.at[h, src],
+            send_sem=gsend.at[h, dst],
+            recv_sem=grecv.at[h, src],
+            device_id={"seq": shard_at(dst)},
+            device_id_type=MESH,
+        )
+
+    first = slab * PLACES
+    later = nplane - first
+    earlier = first + PLACES
+
+    def to_later(k):
+        return first + lax.rem(plane - first + k, later)
+
+    def to_earlier(k):
+        return lax.rem(plane + k, earlier)
+
+    for h in range(heads):
+        swap_copy(h, side).start()
+    for h in range(heads):
+        swap_copy(h, 1 - side).wait_recv()
+
+        def gather_start(k, _, h=h):
+            gather_copy(h, plane, to_later(k)).start()
+            return 0
+
+        lax.fori_loop(1, later, gather_start, 0)
+    for group in loads[2:]:
+        for load in group:
+            load.wait()
 
     rows = 128
     nchunk = total // rows
-    shards = rows // per_dev
+    group = rows // (2 * per_dev)
     lane = lax.broadcasted_iota(jnp.int32, (SPAN, tile), 1)
     low_lane = lax.rem(lane, 2 * SPAN) < SPAN
     causal = lax.broadcasted_iota(jnp.int32, (SPAN, tile), 0) <= lax.rem(lane, SPAN)
@@ -125,6 +166,16 @@
             ]
         return parts[0]
 
+    def term_copy(h, dst, src):
+        return pltpu.make_async_remote_copy(
+            src_ref=term.at[dst, h],
+            dst_ref=rterm.at[src, h],
+            send_sem=rsend.at[h, dst],
+            recv_sem=rrecv.at[h, src],
+            device_id={"seq": shard_at(dst)},
+            device_id_type=MESH,
+        )
+
     def step(n, _):
         h = n // nhead
         j = lax.rem(n, nhead)
@@ -133,13 +184,18 @@
         trow = pl.ds(pl.multiple_of(i * tile, tile), tile)
 
         def sk(c):
-            return summ[c * shards : (c + 1) * shards, 0, :, cols].reshape(rows, HEAD_DIM)
+            return summ[h, c * group : (c + 1) * group, :, 0].reshape(rows, HEAD_DIM)
 
         def sv(c):
-            return summ[c * shards : (c + 1) * shards, 1, :, cols].reshape(rows, HEAD_DIM)
+            return summ[h, c * group : (c + 1) * group, :, 1].reshape(rows, HEAD_DIM)
 
         @pl.when(j == 0)
         def _():
+            def gather_wait(k, _):
+                gather_copy(h, to_earlier(k), plane).wait_recv()
+                return 0
+
+            lax.fori_loop(1, earlier, gather_wait, 0)
             for c in range(nchunk):
                 summ_t[:, c * rows : (c + 1) * rows] = sk(c).astype(F32).T.astype(BF16)
             acc[...] = jnp.zeros(acc.shape, F32)
@@ -164,7 +220,11 @@
             + i * (tile // SPAN)
             + lax.broadcasted_iota(jnp.int32, (rows, tile), 1) // SPAN
         )
-        row_id = lax.broadcasted_iota(jnp.int32, (rows, tile), 0)
+        place_row = lax.broadcasted_iota(jnp.int32, (rows, tile), 0)
+        pair = place_row // per_dev
+        row_id = (
+            (lax.rem(pair, 2) * PLACES + pair // 2) * per_dev + lax.rem(place_row, per_dev)
+        )
         top = fold(a_loc, jnp.maximum)
         for c in range(nchunk):
             s = dot(sk(c), qt, NT)
@@ -231,49 +291,48 @@
         @pl.when(j == nhead - 1)
         def _():
             pltpu.make_async_copy(stage.at[n], out.at[slot], local_sem.at[h]).start()
+            mine = pl.ds(pl.multiple_of(plane * 2 * per_dev, 2 * per_dev), 2 * per_dev)
             for w in range(2):
-                term[:, h, w] = acc[w].reshape(nseq, per_dev, HEAD_DIM).astype(BF16)
-                own[w, :, cols] = acc[w, pl.ds(pl.multiple_of(me * per_dev, per_dev), per_dev)]
+                term[:, h, :, w] = acc[w].reshape(nplane, 2, per_dev, HEAD_DIM).astype(BF16)
+                own[:, h, w] = acc[w, mine].reshape(2, per_dev, HEAD_DIM)
 
             def send_term(k, _):
-                dst = me - 1 - k
-                pltpu.make_async_remote_copy(
-                    src_ref=term.at[dst, h],
-                    dst_ref=rterm.at[me, h],
-                    send_sem=rsend.at[dst],
-                    recv_sem=rrecv.at[me],
-                    device_id={"seq": dst},
-                    device_id_type=MESH,
-                ).start()
+                dst = to_earlier(k)
+                term_copy(h, dst, plane).start()
                 return 0
 
-            lax.fori_loop(0, me, send_term, 0)
+            lax.fori_loop(1, earlier, send_term, 0)
 
         return 0
 
     lax.fori_loop(0, heads * nhead, step, 0)
 
-    def term_all(a, b):
-        return pltpu.make_async_remote_copy(
-            src_ref=term.at[a],
-            dst_ref=rterm.at[b],
-            send_sem=rsend.at[a],
-            recv_sem=rrecv.at[b],
-            device_id={"seq": a},
-            device_id_type=MESH,
-        )
-
-    def add_term(src, _):
-        term_all(0, src).wait_recv()
-        for w in range(2):
-            for h in range(heads):
-                sl = slice(h * HEAD_DIM, (h + 1) * HEAD_DIM)
-                own[w, :, sl] += rterm[src, h, w].astype(F32)
-        return 0
-
-    lax.fori_loop(me + 1, nseq, add_term, 0)
-    grad_k = own[0] * scale
-    grad_v = own[1]
+    for h in range(heads):
+
+        def add_term(k, _, h=h):
+            src = to_later(k)
+            term_copy(h, plane, src).wait_recv()
+            own[:, h] += rterm[src, h].astype(F32)
+            return 0
+
+        lax.fori_loop(1, later, add_term, 0)
+
+    partial = pltpu.make_async_remote_copy(
+        src_ref=own.at[1 - side],
+        dst_ref=other_own,
+        send_sem=psend,
+        recv_sem=precv,
+        device_id={"seq": partner},
+        device_id_type=MESH,
+    )
+    partial.start()
+    partial.wait()
+    grads = [
+        jnp.concatenate([own[side, h, w] + other_own[h, w] for h in range(heads)], axis=1)
+        for w in range(2)
+    ]
+    grad_k = grads[0] * scale
+    grad_v = grads[1]
     gk_out[...] = grad_k
     gv_out[...] = grad_v
     part = per_dev // nhead
@@ -329,29 +388,67 @@
             stage.at[h * nhead + nhead - 1], out.at[hd * heads + h], local_sem.at[h]
         ).wait()
 
-    def gather_sent(dst, _):
-        gather_copy(me, dst).wait_send()
-        return 0
-
-    lax.fori_loop(me + 1, nseq, gather_sent, 0)
-
-    def terms_sent(dst, _):
-        term_all(dst, me).wait_send()
-        return 0
-
-    lax.fori_loop(0, me, terms_sent, 0)
-
-
-def finish_kernel(part, in_ref, shared_ref, q_out, k_out, v_out):
-    heads = in_ref.shape[0]
     for h in range(heads):
-        sl = slice(h * HEAD_DIM, (h + 1) * HEAD_DIM)
-        q_out[:, sl] = in_ref[h, 0]
-        for w, ref in ((0, k_out), (1, v_out)):
-            for c in range(part):
-                rows = slice(c * SPAN, (c + 1) * SPAN)
-                add = shared_ref[0, w * part + c : w * part + c + 1, sl]
-                ref[rows, sl] = (in_ref[h, 1 + w, rows].astype(F32) + add).astype(BF16)
+        swap_copy(h, side).wait_send()
+
+        def gather_sent(k, _, h=h):
+            gather_copy(h, plane, to_later(k)).wait_send()
+            return 0
+
+        def term_sent(k, _, h=h):
+            term_copy(h, to_earlier(k), plane).wait_send()
+            return 0
+
+        lax.fori_loop(1, later, gather_sent, 0)
+        lax.fori_loop(1, earlier, term_sent, 0)
+
+
+def finish_kernel(
+    part, pieces, shared_ref, gk_in, gv_in, q_out, k_out, v_out, gk_out, gv_out, kv, q_buf, k_buf, v_buf, load_sem, sem
+):
+    heads = pieces.shape[0]
+    cols = shared_ref.shape[2]
+    group = cols // HEAD_DIM
+    loads = [
+        pltpu.make_async_copy(pieces.at[h, 1:], kv.at[h], load_sem.at[0, h]) for h in range(heads)
+    ]
+    q_loads = [
+        pltpu.make_async_copy(
+            pieces.at[h, 0], q_buf.at[:, pl.ds(h * HEAD_DIM, HEAD_DIM)], load_sem.at[1, h]
+        )
+        for h in range(heads)
+    ]
+    copies = [
+        pltpu.make_async_copy(gk_in, gk_out, sem.at[0]),
+        pltpu.make_async_copy(gv_in, gv_out, sem.at[1]),
+    ]
+    for q_load, load in zip(q_loads, loads):
+        q_load.start()
+        load.start()
+    for copy in copies:
+        copy.start()
+    for g in range(heads // group):
+        for b in range(group):
+            h = g * group + b
+            q_loads[h].wait()
+            loads[h].wait()
+            for w, buf in ((0, k_buf), (1, v_buf)):
+                for c in range(part):
+                    rows = slice(c * SPAN, (c + 1) * SPAN)
+                    at = w * part + c
+                    add = shared_ref[g, at : at + 1, b * HEAD_DIM : (b + 1) * HEAD_DIM]
+                    buf[rows, h * HEAD_DIM : (h + 1) * HEAD_DIM] = (
+                        kv[h, w, rows].astype(F32) + add
+                    ).astype(BF16)
+        sl = pl.ds(g * cols, cols)
+        for w, (buf, ref) in enumerate(((q_buf, q_out), (k_buf, k_out), (v_buf, v_out))):
+            copy = pltpu.make_async_copy(
+                buf.at[:, sl], ref.at[:, sl], sem.at[2 + 3 * g + w]
+            )
+            copy.start()
+            copies.append(copy)
+    for copy in copies:
+        copy.wait()
 
 
 def per_device(queries, keys, values, out_grad):
@@ -364,7 +461,9 @@
     tile = count // nhead
     part = per_dev // nhead
     steps = heads * nhead
+    nplane = nseq // 2
     anyspace = pl.BlockSpec(memory_space=pl.ANY)
+    hbm = pl.BlockSpec(memory_space=pltpu.HBM)
     vmem = pl.BlockSpec(memory_space=pltpu.VMEM)
     dma = pltpu.SemaphoreType.DMA
     pieces, grad_k, grad_v, shared = pl.pallas_call(
@@ -375,26 +474,31 @@
             jax.ShapeDtypeStruct((per_dev, cols), F32),
             jax.ShapeDtypeStruct((nhead, 2 * part, cols), F32),
         ),
-        in_specs=[anyspace] * 4,
-        out_specs=(anyspace, vmem, vmem, anyspace),
+        in_specs=[hbm] * 4,
+        out_specs=(anyspace, vmem, vmem, vmem),
         scratch_shapes=[pltpu.VMEM((count, cols), BF16)] * 4
         + [
-            pltpu.VMEM((nseq, 2, per_dev, cols), BF16),
+            pltpu.VMEM((heads, nplane, 2, 2, per_dev, HEAD_DIM), BF16),
             pltpu.VMEM((HEAD_DIM, total), BF16),
             pltpu.VMEM((2, total, HEAD_DIM), F32),
-            pltpu.VMEM((nseq, heads, 2, per_dev, HEAD_DIM), BF16),
-            pltpu.VMEM((nseq, heads, 2, per_dev, HEAD_DIM), BF16),
-            pltpu.VMEM((2, per_dev, cols), F32),
+            pltpu.VMEM((nplane, heads, 2, 2, per_dev, HEAD_DIM), BF16),
+            pltpu.VMEM((nplane, heads, 2, 2, per_dev, HEAD_DIM), BF16),
+            pltpu.VMEM((2, heads, 2, per_dev, HEAD_DIM), F32),
+            pltpu.VMEM((heads, 2, per_dev, HEAD_DIM), F32),
             pltpu.VMEM((nhead, 2 * part, cols), F32),
             pltpu.VMEM((steps, 3, tile, HEAD_DIM), BF16),
             pltpu.VMEM((total, tile), F32),
             pltpu.VMEM((total, tile), F32),
             pltpu.VMEM((total, tile), F32),
-            dma((4,)),
-            dma((nseq,)),
-            dma((nseq,)),
-            dma((nseq,)),
-            dma((nseq,)),
+            dma((4, nhead)),
+            dma((heads,)),
+            dma((heads,)),
+            dma((heads, nplane)),
+            dma((heads, nplane)),
+            dma((heads, nplane)),
+            dma((heads, nplane)),
+            dma,
+            dma,
             dma((steps,)),
             dma((nhead,)),
             dma((heads,)),
@@ -403,23 +507,28 @@
             dma,
         ],
         compiler_params=pltpu.CompilerParams(
-            collective_id=0, has_side_effects=True, vmem_limit_bytes=40 * 1024 * 1024
+            collective_id=0, has_side_effects=True, vmem_limit_bytes=53 * 1024 * 1024
         ),
         name="attend",
     )(queries, keys, values, out_grad)
     row = jax.ShapeDtypeStruct((tile, nhead * cols), BF16)
-    col_block = pl.BlockSpec((tile, cols), lambda g: (0, g))
-    query_grad, key_grad, value_grad = pl.pallas_call(
+    block = jax.ShapeDtypeStruct((per_dev, cols), F32)
+    query_grad, key_grad, value_grad, grad_k, grad_v = pl.pallas_call(
         functools.partial(finish_kernel, part),
-        out_shape=(row, row, row),
-        grid=(nhead,),
-        in_specs=[
-            pl.BlockSpec((heads, 3, tile, HEAD_DIM), lambda g: (g, 0, 0, 0)),
-            pl.BlockSpec((1, 2 * part, cols), lambda g: (g, 0, 0)),
+        out_shape=(row, row, row, block, block),
+        in_specs=[hbm, vmem, vmem, vmem],
+        out_specs=(hbm,) * 5,
+        scratch_shapes=[
+            pltpu.VMEM((nhead * heads, 2, tile, HEAD_DIM), BF16),
+            pltpu.VMEM((tile, nhead * cols), BF16),
+            pltpu.VMEM((tile, nhead * cols), BF16),
+            pltpu.VMEM((tile, nhead * cols), BF16),
+            dma((2, nhead * heads)),
+            dma((2 + 3 * nhead,)),
         ],
-        out_specs=(col_block, col_block, col_block),
+        compiler_params=pltpu.CompilerParams(vmem_limit_bytes=53 * 1024 * 1024),
         name="finish",
-    )(pieces, shared)
+    )(pieces, shared, grad_k, grad_v)
     return (query_grad, key_grad, value_grad, grad_k, grad_v)
 
 

time: 94.5 us -> 64.2 us (0.68)
  Pallas kernels: 85.1 us -> 63.4 us
  local copies, waits for them, and re-layouts: 8.37 us -> 0 us
    pallas_call x1, Pallas kernels: 80.9 us -> 60.1 us  [per_device(): pl.pallas_call(functools.partial(main_kernel, nseq, nhead), out_shape=(ja...]
    unnamed x14 -> x0, local copies, waits for them, and re-layouts: 8.37 us -> none
    pallas_call x1, Pallas kernels: 4.24 us -> 3.29 us  [per_device(): pl.pallas_call(functools.partial(finish_kernel, part), out_shape=(row, ro...]
where the time goes in v2:
time: 64.2 us; the launch traced here: 64.1 us
  Pallas kernels  63.4 us (99%)
    pallas_call x1, Pallas kernels, per_device(): pl.pallas_call(functools.partial(main_kernel, nseq, nhead), out_shape=(ja...  60.1 us
    pallas_call x1, Pallas kernels, per_device(): pl.pallas_call(functools.partial(finish_kernel, part), out_shape=(row, ro...  3.29 us

profile of v2, /device:TPU:1, one launch (start us, length us, event | category | flops | bytes accessed | tf_op | source)
XLA Modules:
  0.0 64.1 jit_solution(8483976320765282660)
XLA Ops:
  0.6 60.1 %attend.1 = (bf16[16,3,256,128]{3,2,1,0:T(8,128)(2,1)}, f32[16,512]{1,0:T(8,128)S(1)}, f32[16,512]{1,0:T(8,128)S(1)}, f32[4,8,512]{2,1,0:T(8,128)S(1)}) custom-call(bf16[1024,512]{1,0:T(8,128)(2,1)} %q_hbm.1, bf16[1024,512]{1,0:T(8,128)(2,1)} %k_hbm.1, bf16[1024,512]{1,0:T(8,128)(2,1)} %v_hbm.1, bf16[1024,512]{1,0:T(8,128)(2,1)} %d_hbm.1), custom_call_target="tpu_custom_call" | custom-call | tf_op jit(solution)/shard_map/attend/pallas_call | solution.py:469
  60.8 3.3 %finish.1 = (bf16[256,2048]{1,0:T(8,128)(2,1)}, bf16[256,2048]{1,0:T(8,128)(2,1)}, bf16[256,2048]{1,0:T(8,128)(2,1)}, f32[16,512]{1,0:T(8,128)}, f32[16,512]{1,0:T(8,128)}) custom-call(bf16[16,3,256,128]{3,2,1,0:T(8,128)(2,1)} %get-tuple-element.9.pieces, f32[4,8,512]{2,1,0:T(8,128)S(1)} %get-tuple-element.10.shared_ref, ...), custom_call_target="tpu_custom_call" | custom-call | tf_op jit(solution)/shard_map/finish/pallas_call | solution.py:516

commit v3 on v2

--- a/solution.py
+++ b/solution.py
@@ -88,9 +88,13 @@
     lax.fori_loop(1, nplane, greet, 0)
     pl.semaphore_signal(barrier, inc=1, device_id={"seq": partner}, device_id_type=MESH)
     for i in range(1, nhead):
-        pl.semaphore_signal(
-            barrier, inc=1, device_id={"head": lax.rem(hd + i, nhead)}, device_id_type=MESH
-        )
+        for shard in (me, partner):
+            pl.semaphore_signal(
+                barrier,
+                inc=1,
+                device_id={"seq": shard, "head": lax.rem(hd + i, nhead)},
+                device_id_type=MESH,
+            )
 
     pool = (
         lax.broadcasted_iota(jnp.int32, (per_dev, count), 1) // SPAN
@@ -103,7 +107,7 @@
         for h in range(heads):
             summ[h, plane, side, w] = mean[:, h * HEAD_DIM : (h + 1) * HEAD_DIM]
 
-    pl.semaphore_wait(barrier, nplane - 1 + 1 + nhead - 1)
+    pl.semaphore_wait(barrier, nplane - 1 + 1 + 2 * (nhead - 1))
 
     def swap_copy(h, to):
         return pltpu.make_async_remote_copy(
@@ -175,6 +179,25 @@
             device_id={"seq": shard_at(dst)},
             device_id_type=MESH,
         )
+
+    def tile_copy(n, to):
+        return pltpu.make_async_remote_copy(
+            src_ref=stage.at[n],
+            dst_ref=out.at[hd * heads + n // nhead],
+            send_sem=asend.at[n],
+            recv_sem=arecv.at[hd],
+            device_id={"head": to},
+            device_id_type=MESH,
+        )
+
+    def cross(m):
+        return nhead * (m // 2) + lax.rem(m, 2)
+
+    def send_cross(m):
+        tile_copy(cross(m), tile_order(hd, lax.rem(m, 2))).start()
+
+    def wait_cross(m):
+        tile_copy(cross(m), tile_order(hd, lax.rem(m, 2))).wait_send()
 
     def step(n, _):
         h = n // nhead
@@ -275,22 +298,25 @@
             dqt = dqt + dot(summ_t[:, sl], g, NN)
         stage[n, 0] = (dqt * scale).T.astype(BF16)
 
-        slot = hd * heads + h
-
-        @pl.when(j < nhead - 1)
+        @pl.when(n == 0)
         def _():
-            pltpu.make_async_remote_copy(
-                src_ref=stage.at[n],
-                dst_ref=out.at[slot],
-                send_sem=asend.at[n],
-                recv_sem=arecv.at[hd],
-                device_id={"head": i},
-                device_id_type=MESH,
-            ).start()
+            send_cross(0)
+
+        @pl.when(j == 1)
+        def _():
+            @pl.when(h >= 1)
+            def _():
+                wait_cross(h - 1)
+
+            send_cross(h + 1)
+
+        @pl.when(j == 2)
+        def _():
+            tile_copy(n, i).start()
 
         @pl.when(j == nhead - 1)
         def _():
-            pltpu.make_async_copy(stage.at[n], out.at[slot], local_sem.at[h]).start()
+            pltpu.make_async_copy(stage.at[n], out.at[hd * heads + h], local_sem.at[h]).start()
             mine = pl.ds(pl.multiple_of(plane * 2 * per_dev, 2 * per_dev), 2 * per_dev)
             for w in range(2):
                 term[:, h, :, w] = acc[w].reshape(nplane, 2, per_dev, HEAD_DIM).astype(BF16)
@@ -307,6 +333,8 @@
 
     lax.fori_loop(0, heads * nhead, step, 0)
 
+    send_cross(heads + 1)
+    send_cross(heads + 2)
     for h in range(heads):
 
         def add_term(k, _, h=h):
@@ -317,48 +345,75 @@
 
         lax.fori_loop(1, later, add_term, 0)
 
+    part = per_dev // nhead
+    half = heads // 2
+
+    def sums_of(which, w):
+        factor = scale if w == 0 else 1.0
+        return [own[which, h, w] * factor for h in range(heads)]
+
+    def share_of(blocks, dst):
+        rows_of = slice(dst * part, (dst + 1) * part)
+        pieces = [
+            jnp.concatenate([blocks[w][b * half + a][rows_of] for a in range(half)], axis=1)
+            for w in range(2)
+            for b in range(2)
+        ]
+        return (jnp.concatenate(pieces, axis=0) * (1.0 / SPAN)).astype(BF16)
+
+    mine = [sums_of(side, w) for w in range(2)]
+    theirs = [sums_of(1 - side, w) for w in range(2)]
+    for w in range(2):
+        for h in range(heads):
+            other_own[0, h, w] = theirs[w][h].astype(BF16)
     partial = pltpu.make_async_remote_copy(
-        src_ref=own.at[1 - side],
-        dst_ref=other_own,
+        src_ref=other_own.at[0],
+        dst_ref=other_own.at[1],
         send_sem=psend,
         recv_sem=precv,
         device_id={"seq": partner},
         device_id_type=MESH,
     )
     partial.start()
-    partial.wait()
-    grads = [
-        jnp.concatenate([own[side, h, w] + other_own[h, w] for h in range(heads)], axis=1)
-        for w in range(2)
-    ]
-    grad_k = grads[0] * scale
-    grad_v = grads[1]
-    gk_out[...] = grad_k
-    gv_out[...] = grad_v
-    part = per_dev // nhead
     for dst in range(nhead):
-        sgs[dst, 0:part] = grad_k[dst * part : (dst + 1) * part] * (1.0 / SPAN)
-        sgs[dst, part : 2 * part] = grad_v[dst * part : (dst + 1) * part] * (1.0 / SPAN)
-
-    def shared_copy(src, dst, slot):
+        sgs[0, dst] = share_of(mine, dst)
+        sgs[1, dst] = share_of(theirs, dst)
+
+    def shared_copy(at, shard, from_side, src, dst):
         return pltpu.make_async_remote_copy(
-            src_ref=sgs.at[dst],
-            dst_ref=shared.at[src],
-            send_sem=ssend.at[slot],
-            recv_sem=srecv.at[src],
-            device_id={"head": dst},
-            device_id_type=MESH,
-        )
-
-    for k in range(1, nhead):
-        shared_copy(hd, lax.rem(hd + k, nhead), k).start()
-    mine = pltpu.make_async_copy(sgs.at[hd], shared.at[hd], own_sem)
-    mine.start()
-    mine.wait()
+            src_ref=sgs.at[at, dst],
+            dst_ref=shared.at[from_side, src],
+            send_sem=ssend.at[at, dst],
+            recv_sem=srecv.at[from_side, src],
+            device_id={"seq": shard, "head": dst},
+            device_id_type=MESH,
+        )
+
     for k in range(1, nhead):
         other = lax.rem(hd + k, nhead)
-        shared_copy(hd, other, k).wait_send()
-        shared_copy(other, other, k).wait_recv()
+        shared_copy(1, partner, side, hd, other).start()
+        shared_copy(0, me, side, hd, other).start()
+    for m in range(heads + 3, 2 * heads):
+        send_cross(m)
+    keep = pltpu.make_async_copy(sgs.at[0, hd], shared.at[side, hd], own_sem)
+    keep.start()
+    keep.wait()
+    partial.wait()
+    arrived = [[other_own[1, h, w].astype(F32) for h in range(heads)] for w in range(2)]
+    gk_out[...] = jnp.concatenate([mine[0][h] + arrived[0][h] for h in range(heads)], axis=1)
+    gv_out[...] = jnp.concatenate([mine[1][h] + arrived[1][h] for h in range(heads)], axis=1)
+    for dst in range(nhead):
+
+        @pl.when(hd == dst)
+        def _():
+            shared[1 - side, dst] = share_of(arrived, dst)
+
+    for k in range(1, nhead):
+        other = lax.rem(hd + k, nhead)
+        for at, shard in ((1, partner), (0, me)):
+            shared_copy(at, shard, side, hd, other).wait_send()
+        for from_side in range(2):
+            shared_copy(0, me, from_side, other, other).wait_recv()
         pltpu.make_async_remote_copy(
             src_ref=stage.at[0],
             dst_ref=out.at[pl.ds(other * heads, heads)],
@@ -368,21 +423,10 @@
             device_id_type=MESH,
         ).wait_recv()
 
-    def sent_all(n, _):
-        @pl.when(lax.rem(n, nhead) < nhead - 1)
-        def _():
-            pltpu.make_async_remote_copy(
-                src_ref=stage.at[n],
-                dst_ref=out.at[0],
-                send_sem=asend.at[n],
-                recv_sem=arecv.at[hd],
-                device_id={"head": lax.rem(hd + 1, nhead)},
-                device_id_type=MESH,
-            ).wait_send()
-
-        return 0
-
-    lax.fori_loop(0, heads * nhead, sent_all, 0)
+    for m in range(heads - 1, 2 * heads):
+        wait_cross(m)
+    for h in range(heads):
+        tile_copy(h * nhead + 2, tile_order(hd, 2)).wait_send()
     for h in range(heads):
         pltpu.make_async_copy(
             stage.at[h * nhead + nhead - 1], out.at[hd * heads + h], local_sem.at[h]
@@ -407,7 +451,7 @@
     part, pieces, shared_ref, gk_in, gv_in, q_out, k_out, v_out, gk_out, gv_out, kv, q_buf, k_buf, v_buf, load_sem, sem
 ):
     heads = pieces.shape[0]
-    cols = shared_ref.shape[2]
+    cols = 2 * shared_ref.shape[3]
     group = cols // HEAD_DIM
     loads = [
         pltpu.make_async_copy(pieces.at[h, 1:], kv.at[h], load_sem.at[0, h]) for h in range(heads)
@@ -427,6 +471,9 @@
         load.start()
     for copy in copies:
         copy.start()
+    shares = [
+        shared_ref[0, g].astype(F32) + shared_ref[1, g].astype(F32) for g in range(heads // group)
+    ]
     for g in range(heads // group):
         for b in range(group):
             h = g * group + b
@@ -435,8 +482,9 @@
             for w, buf in ((0, k_buf), (1, v_buf)):
                 for c in range(part):
                     rows = slice(c * SPAN, (c + 1) * SPAN)
-                    at = w * part + c
-                    add = shared_ref[g, at : at + 1, b * HEAD_DIM : (b + 1) * HEAD_DIM]
+                    at = (2 * w + b // 2) * part + c
+                    sl = slice((b % 2) * HEAD_DIM, (b % 2 + 1) * HEAD_DIM)
+                    add = shares[g][at : at + 1, sl]
                     buf[rows, h * HEAD_DIM : (h + 1) * HEAD_DIM] = (
                         kv[h, w, rows].astype(F32) + add
                     ).astype(BF16)
@@ -472,7 +520,7 @@
             jax.ShapeDtypeStruct((nhead * heads, 3, tile, HEAD_DIM), BF16),
             jax.ShapeDtypeStruct((per_dev, cols), F32),
             jax.ShapeDtypeStruct((per_dev, cols), F32),
-            jax.ShapeDtypeStruct((nhead, 2 * part, cols), F32),
+            jax.ShapeDtypeStruct((2, nhead, 4 * part, cols // 2), BF16),
         ),
         in_specs=[hbm] * 4,
         out_specs=(anyspace, vmem, vmem, vmem),
@@ -484,8 +532,8 @@
             pltpu.VMEM((nplane, heads, 2, 2, per_dev, HEAD_DIM), BF16),
             pltpu.VMEM((nplane, heads, 2, 2, per_dev, HEAD_DIM), BF16),
             pltpu.VMEM((2, heads, 2, per_dev, HEAD_DIM), F32),
-            pltpu.VMEM((heads, 2, per_dev, HEAD_DIM), F32),
-            pltpu.VMEM((nhead, 2 * part, cols), F32),
+            pltpu.VMEM((2, heads, 2, per_dev, HEAD_DIM), BF16),
+            pltpu.VMEM((2, nhead, 4 * part, cols // 2), BF16),
             pltpu.VMEM((steps, 3, tile, HEAD_DIM), BF16),
             pltpu.VMEM((total, tile), F32),
             pltpu.VMEM((total, tile), F32),
@@ -502,8 +550,8 @@
             dma((steps,)),
             dma((nhead,)),
             dma((heads,)),
-            dma((nhead,)),
-            dma((nhead,)),
+            dma((2, nhead)),
+            dma((2, nhead)),
             dma,
         ],
         compiler_params=pltpu.CompilerParams(

time: 64.2 us -> 60.4 us (0.941)
  Pallas kernels: 63.4 us -> 59.6 us
    pallas_call x1, Pallas kernels: 60.1 us -> 56.3 us  [per_device(): pl.pallas_call(functools.partial(main_kernel, nseq, nhead), out_shape=(ja...]
where the time goes in v3:
time: 60.4 us; the launch traced here: 60.2 us
  Pallas kernels  59.6 us (99%)
  between operations  0.64 us (1%)
    pallas_call x1, Pallas kernels, per_device(): pl.pallas_call(functools.partial(main_kernel, nseq, nhead), out_shape=(ja...  56.3 us
    pallas_call x1, Pallas kernels, per_device(): pl.pallas_call(functools.partial(finish_kernel, part), out_shape=(row, ro...  3.29 us

profile of v3, /device:TPU:1, one launch (start us, length us, event | category | flops | bytes accessed | tf_op | source)
XLA Modules:
  0.0 60.2 jit_solution(5376104336238749847)
XLA Ops:
  0.6 56.3 %attend.1 = (bf16[16,3,256,128]{3,2,1,0:T(8,128)(2,1)}, f32[16,512]{1,0:T(8,128)S(1)}, f32[16,512]{1,0:T(8,128)S(1)}, bf16[2,4,16,256]{3,2,1,0:T(8,128)(2,1)S(1)}) custom-call(bf16[1024,512]{1,0:T(8,128)(2,1)} %q_hbm.1, bf16[1024,512]{1,0:T(8,128)(2,1)} %k_hbm.1, bf16[1024,512]{1,0:T(8,128)(2,1)} %v_hbm.1, bf16[1024,512]{1,0:T(8,128)(2,1)} %d_hbm.1), custom_call_target="tpu_custom_call" | custom-call | tf_op jit(solution)/shard_map/attend/pallas_call | solution.py:517
  56.9 3.3 %finish.1 = (bf16[256,2048]{1,0:T(8,128)(2,1)}, bf16[256,2048]{1,0:T(8,128)(2,1)}, bf16[256,2048]{1,0:T(8,128)(2,1)}, f32[16,512]{1,0:T(8,128)}, f32[16,512]{1,0:T(8,128)}) custom-call(bf16[16,3,256,128]{3,2,1,0:T(8,128)(2,1)} %get-tuple-element.9.pieces, bf16[2,4,16,256]{3,2,1,0:T(8,128)(2,1)S(1)} %get-tuple-element.10.shared_ref, ...), custom_call_target="tpu_custom_call" | custom-call | tf_op jit(solution)/shard_map/finish/pallas_call | solution.py:564

commit v4 on v3

v4 whole, which is shorter than its diff:
```python
import functools

import jax
import jax.numpy as jnp
from jax import lax
from jax.experimental import pallas as pl
from jax.experimental.pallas import tpu as pltpu
from jax.sharding import PartitionSpec as P

HEAD_DIM = 128
SPAN = 64
PLACES = 4
SLAB = 8
EARLY = 2
MESH = pl.DeviceIdType.MESH
LOG2E = 1.4426950408889634
F32 = jnp.float32
BF16 = jnp.bfloat16
NT = (((1,), (1,)), ((), ()))
NN = (((1,), (0,)), ((), ()))
TN = (((0,), (0,)), ((), ()))


def dot(a, b, dims):
    return lax.dot_general(a, b, dims, preferred_element_type=F32)


def main_kernel(
    nseq,
    nhead,
    q_hbm, k_hbm, v_hbm, d_hbm,
    out, gk_out, gv_out, shared, tri,
    q_ref, k_ref, v_ref, d_ref,
    sumk, sumv, summ_t, acc, term, rterm, own, other_own, sgs, stage, tri_stage, s_scr, dp_scr,
    load_sem, xsend, xrecv, gsend, grecv, rsend, rrecv, psend, precv,
    asend, arecv, local_sem, ssend, srecv, own_sem, esend, tsend, trecv,
):
    me = lax.axis_index("seq")
    hd = lax.axis_index("head")
    count = q_ref.shape[0]
    heads = q_ref.shape[1] // HEAD_DIM
    per_dev = count // SPAN
    total = per_dev * nseq
    tile = count // nhead
    scale = HEAD_DIM ** (-0.5)
    c2 = scale * LOG2E
    slab = me // SLAB
    side = lax.rem(me, SLAB) // PLACES
    place = lax.rem(me, PLACES)
    plane = slab * PLACES + place
    nplane = nseq // 2
    partner = me + PLACES - 2 * PLACES * side

    def shard_at(p):
        return (p // PLACES) * SLAB + side * PLACES + lax.rem(p, PLACES)

    loads = [
        [
            pltpu.make_async_copy(
                src.at[c * tile : (c + 1) * tile], dst.at[c * tile : (c + 1) * tile], load_sem.at[i, c]
            )
            for c in range(nhead)
        ]
        for i, (src, dst) in enumerate(
            ((k_hbm, k_ref), (v_hbm, v_ref), (q_hbm, q_ref), (d_hbm, d_ref))
        )
    ]
    for group in loads:
        for load in group:
            load.start()
    sumk[...] = jnp.zeros(sumk.shape, sumk.dtype)
    sumv[...] = jnp.zeros(sumv.shape, sumv.dtype)
    rterm[...] = jnp.zeros(rterm.shape, rterm.dtype)

    barrier = pltpu.get_barrier_semaphore()

    def greet(i, _):
        pl.semaphore_signal(
            barrier,
            inc=1,
            device_id={"seq": shard_at(lax.rem(plane + i, nplane))},
            device_id_type=MESH,
        )
        return 0

    lax.fori_loop(1, nplane, greet, 0)
    pl.semaphore_signal(barrier, inc=1, device_id={"seq": partner}, device_id_type=MESH)
    for i in range(1, nhead):
        for shard in (me, partner):
            pl.semaphore_signal(
                barrier,
                inc=1,
                device_id={"seq": shard, "head": lax.rem(hd + i, nhead)},
                device_id_type=MESH,
            )

    pool = (
        lax.broadcasted_iota(jnp.int32, (per_dev, count), 1) // SPAN
        == lax.broadcasted_iota(jnp.int32, (per_dev, count), 0)
    ).astype(BF16)
    for w, ref in ((0, k_ref), (1, v_ref)):
        for load in loads[w]:
            load.wait()
        mean = (dot(pool, ref[...], NN) * (1.0 / SPAN)).astype(BF16)
        for h in range(heads):
            block = mean[:, h * HEAD_DIM : (h + 1) * HEAD_DIM]
            if w == 0:
                sumk[h, slab, place, side] = block
            else:
                sumv[h, place, slab, side] = block

    pl.semaphore_wait(barrier, nplane - 1 + 1 + 2 * (nhead - 1))

    slabs = nplane // PLACES

    def swap_copy(w, to):
        ref = sumk.at[:, slab, place, to] if w == 0 else sumv.at[:, place, slab, to]
        return pltpu.make_async_remote_copy(
            src_ref=ref,
            dst_ref=ref,
            send_sem=xsend.at[w],
            recv_sem=xrecv.at[w],
            device_id={"seq": partner},
            device_id_type=MESH,
        )

    def gather_copy(kind, h, src, dst):
        ref = (
            sumk.at[h, slab, src],
            sumv.at[h, place, src],
            sumk.at[h, src],
            sumv.at[h, src],
        )[kind]
        to_place = kind in (0, 3)
        shard = slab * SLAB + side * PLACES + dst if to_place else dst * SLAB + side * PLACES + place
        return pltpu.make_async_remote_copy(
            src_ref=ref,
            dst_ref=ref,
            send_sem=gsend.at[kind, h, dst],
            recv_sem=grecv.at[kind, h, src],
            device_id={"seq": shard},
            device_id_type=MESH,
        )

    def gather_each(kind, h, what):
        def go(other, _):
            if what == "start":
                gather_copy(kind, h, mine_of, other).start()
            elif what == "sent":
                gather_copy(kind, h, mine_of, other).wait_send()
            else:
                gather_copy(kind, h, other, mine_of).wait_recv()
            return 0

        if kind in (0, 3):
            mine_of = place
            for k in range(1, PLACES):
                go(lax.rem(place + k, PLACES), 0)
        else:
            mine_of = slab
            if what == "arrived":
                lax.fori_loop(0, slab, go, 0)
            else:
                lax.fori_loop(slab + 1, slabs, go, 0)

    first = slab * PLACES
    later = nplane - first
    earlier = first + PLACES

    def to_later(k):
        return first + lax.rem(plane - first + k, later)

    def to_earlier(k):
        return lax.rem(plane + k, earlier)

    for w in range(2):
        swap_copy(w, side).start()
    for group in loads[2:]:
        for load in group:
            load.wait()

    plain = heads - EARLY

    other_chip = (1 - hd // 2) * 2

    def early_copy(e, j, w):
        ref = (q_ref, d_ref)[w]
        to = other_chip + j
        cols = slice((plain + e) * HEAD_DIM, (plain + e + 1) * HEAD_DIM)
        return pltpu.make_async_remote_copy(
            src_ref=ref.at[pl.ds(pl.multiple_of(to * tile, tile), tile), cols],
            dst_ref=out.at[hd * heads + plain + e, 1 + w],
            send_sem=esend.at[e, j, w],
            recv_sem=arecv.at[hd],
            device_id={"head": to},
            device_id_type=MESH,
        )

    early = [early_copy(e, j, w) for e in range(EARLY) for j in range(2) for w in range(2)]
    for copy in early:
        copy.start()
    for w in range(2):
        swap_copy(w, 1 - side).wait_recv()
    for h in range(heads):
        for kind in (0, 1):
            gather_each(kind, h, "start")
    for h in range(heads):
        for kind in (0, 1):
            gather_each(kind, h, "arrived")
            gather_each(kind + 2, h, "start")

    rows = 128
    nchunk = total // rows
    lane = lax.broadcasted_iota(jnp.int32, (SPAN, tile), 1)
    low_lane = lax.rem(lane, 2 * SPAN) < SPAN
    causal = lax.broadcasted_iota(jnp.int32, (SPAN, tile), 0) <= lax.rem(lane, SPAN)
    low128 = low_lane[:, : 2 * SPAN]
    diagonal = (lax.broadcasted_iota(jnp.int32, (SPAN, tile), 0) == lax.rem(lane, SPAN))[:, : 2 * SPAN]
    eye = (
        lax.broadcasted_iota(jnp.int32, (2 * SPAN, 2 * SPAN), 0)
        == lax.broadcasted_iota(jnp.int32, (2 * SPAN, 2 * SPAN), 1)
    ).astype(BF16)

    def fold(x, op):
        parts = [x[8 * i : 8 * i + 8] for i in range(x.shape[0] // 8)]
        while len(parts) > 1:
            parts = [
                op(parts[i], parts[i + 1]) if i + 1 < len(parts) else parts[i]
                for i in range(0, len(parts), 2)
            ]
        return parts[0]

    def term_copy(h, dst, src):
        return pltpu.make_async_remote_copy(
            src_ref=term.at[dst, h],
            dst_ref=rterm.at[src, h],
            send_sem=rsend.at[h, dst],
            recv_sem=rrecv.at[h, src],
            device_id={"seq": shard_at(dst)},
            device_id_type=MESH,
        )

    def tile_copy(h, to):
        return pltpu.make_async_remote_copy(
            src_ref=stage.at[h, to],
            dst_ref=out.at[hd * heads + h],
            send_sem=asend.at[h, to],
            recv_sem=arecv.at[hd],
            device_id={"head": to},
            device_id_type=MESH,
        )

    def cross_copies(m, packed):
        h = m // 2
        to = other_chip + lax.rem(m, 2)
        if not packed:
            return [tile_copy(h, to)]
        e = h - plain
        return [
            pltpu.make_async_remote_copy(
                src_ref=tri_stage.at[e, lax.rem(m, 2)],
                dst_ref=tri.at[lax.rem(hd, 2), e],
                send_sem=tsend.at[m - 2 * plain],
                recv_sem=trecv.at[lax.rem(hd, 2)],
                device_id={"head": to},
                device_id_type=MESH,
            ),
            pltpu.make_async_remote_copy(
                src_ref=stage.at[h, to, 0],
                dst_ref=out.at[hd * heads + h, 0],
                send_sem=asend.at[h, to],
                recv_sem=arecv.at[hd],
                device_id={"head": to},
                device_id_type=MESH,
            ),
        ]

    def send_cross(m):
        for packed in (False, True):

            @pl.when((m >= 2 * plain) == packed)
            def _():
                for copy in cross_copies(m, packed):
                    copy.start()

    def wait_cross(m):
        for packed in (False, True):

            @pl.when((m >= 2 * plain) == packed)
            def _():
                for copy in cross_copies(m, packed):
                    copy.wait_send()

    def add_terms(h):
        def term_wait(k, _):
            term_copy(h, plane, to_later(k)).wait_recv()
            return 0

        lax.fori_loop(1, later, term_wait, 0)
        total_own = own[:, h]
        for src in range(nplane):
            total_own = total_own + rterm[src, h].astype(F32)
        own[:, h] = total_own

    place_row = lax.broadcasted_iota(jnp.int32, (rows, tile), 0)
    pair_of = place_row // per_dev
    row_id = (
        (lax.rem(pair_of, 2) * PLACES + pair_of // 2) * per_dev + lax.rem(place_row, per_dev)
    )
    lane_span = lax.broadcasted_iota(jnp.int32, (rows, tile), 1) // SPAN
    zero = jnp.zeros((SPAN, 2 * SPAN), F32)

    def step(n, _):
        h = n // 2
        own_chip = lax.rem(n, 2)
        chip = lax.rem(hd // 2 + 1 + own_chip, 2)
        cols = pl.ds(pl.multiple_of(h * HEAD_DIM, HEAD_DIM), HEAD_DIM)

        def sk(c):
            return sumk[h, c].reshape(rows, HEAD_DIM)

        def sv(c):
            return sumv[h, :, c].reshape(rows, HEAD_DIM)

        @pl.when(own_chip == 0)
        def _():
            for kind in (2, 3):
                gather_each(kind, h, "arrived")
            for c in range(nchunk):
                summ_t[:, c * rows : (c + 1) * rows] = sk(c).astype(F32).T.astype(BF16)
            acc[...] = jnp.zeros(acc.shape, F32)

        def local(a, b):
            picked = []
            for p in range(tile // (2 * SPAN)):
                sl = slice(p * 2 * SPAN, (p + 1) * 2 * SPAN)
                full = dot(a[sl], b[sl], NT)
                picked.append(jnp.where(low128, full[:SPAN], full[SPAN:]))
            return jnp.concatenate(picked, axis=1)

        tri_at = jnp.where((h >= plain) & (own_chip == 0), h - plain, EARLY)
        q, k, v, d, base, top, inv, delta, p_loc, a_loc, dp_loc, dqt = ([None, None] for _ in range(12))

        def scores(t):
            trow = pl.ds(pl.multiple_of((chip * 2 + t) * tile, tile), tile)
            q[t], k[t], v[t], d[t] = (r[trow, cols] for r in (q_ref, k_ref, v_ref, d_ref))
            a_loc[t] = jnp.where(causal, local(k[t], q[t]), -jnp.inf)
            most = fold(a_loc[t], jnp.maximum)
            span_of = me * per_dev + (chip * 2 + t) * (tile // SPAN) + lane_span
            for c in range(nchunk):
                x = dot(sk(c), q[t], NT)
                x = jnp.where(row_id + c * rows < span_of, x, -jnp.inf)
                s_scr[t, c * rows : (c + 1) * rows] = x
                most = jnp.maximum(most, fold(x, jnp.maximum))
            base[t] = jnp.max(most, axis=0, keepdims=True) * c2

        def weights(t):
            dp_loc[t] = local(v[t], d[t])
            e_loc = jnp.exp2(a_loc[t] * c2 - base[t])
            mass = fold(e_loc, jnp.add)
            weighted = fold(e_loc * dp_loc[t], jnp.add)
            for c in range(nchunk):
                sl = slice(c * rows, (c + 1) * rows)
                dp = dot(sv(c), d[t], NT)
                e = jnp.exp2(s_scr[t, sl] * c2 - base[t])
                s_scr[t, sl] = e
                dp_scr[t, sl] = dp
                mass = mass + fold(e, jnp.add)
                weighted = weighted + fold(e * dp, jnp.add)
            inv[t] = 1.0 / jnp.sum(mass, axis=0, keepdims=True)
            delta[t] = jnp.sum(weighted, axis=0, keepdims=True) * inv[t]
            p_loc[t] = e_loc * inv[t]

        def local_grads(t):
            to = chip * 2 + t
            g_loc = p_loc[t] * (dp_loc[t] - delta[t])
            parts = []
            for p in range(tile // (2 * SPAN)):
                sl = slice(p * 2 * SPAN, (p + 1) * 2 * SPAN)
                g = g_loc[:, sl]
                w = p_loc[t][:, sl]
                g2 = jnp.concatenate(
                    [jnp.where(low128, g, zero), jnp.where(low128, zero, g)], axis=0
                ).astype(BF16)
                w2 = jnp.concatenate(
                    [jnp.where(low128, w, zero), jnp.where(low128, zero, w)], axis=0
                ).astype(BF16)
                stage[h, to, 1, sl] = (dot(g2, q[t][sl], NN) * scale).astype(BF16)
                stage[h, to, 2, sl] = dot(w2, d[t][sl], NN).astype(BF16)
                turned = dot(eye, w2, NT)
                turned = jnp.where(low128, turned[:SPAN], turned[SPAN:])
                tri_stage[tri_at, t, :SPAN, sl] = jnp.where(causal[:, sl], g, turned).astype(BF16)
                main = jnp.sum(jnp.where(diagonal, w, zero), axis=0, keepdims=True)
                tri_stage[tri_at, t, SPAN:, sl] = jnp.broadcast_to(main, (16, 2 * SPAN)).astype(BF16)
                parts.append(dot(k[t][sl], g2, TN))
            dqt[t] = jnp.concatenate(parts, axis=1)

        for t in range(2):
            scores(t)
        for t in range(2):
            weights(t)
        for t in range(2):
            local_grads(t)
        for c in range(nchunk):
            sl = slice(c * rows, (c + 1) * rows)
            for t in range(2):
                r = s_scr[t, sl] * inv[t]
                g = (r * (dp_scr[t, sl] - delta[t])).astype(BF16)
                add_k = dot(g, q[t], NN)
                add_v = dot(r.astype(BF16), d[t], NN)
                sum_k, sum_v = (add_k, add_v) if t == 0 else (sum_k + add_k, sum_v + add_v)
                dqt[t] = dqt[t] + dot(summ_t[:, sl], g, NN)
            acc[0, sl] += sum_k
            acc[1, sl] += sum_v
        for t in range(2):
            stage[h, chip * 2 + t, 0] = (dqt[t] * scale).T.astype(BF16)

        @pl.when(own_chip == 0)
        def _():
            @pl.when(h == 0)
            def _():
                send_cross(0)

            @pl.when(h >= 1)
            def _():
                wait_cross(h - 1)

            send_cross(h + 1)


        @pl.when(own_chip == 1)
        def _():
            tile_copy(h, hd + 1 - 2 * lax.rem(hd, 2)).start()
            pltpu.make_async_copy(stage.at[h, hd], out.at[hd * heads + h], local_sem.at[h]).start()
            mine = pl.ds(pl.multiple_of(plane * 2 * per_dev, 2 * per_dev), 2 * per_dev)
            for w in range(2):
                term[:, h, :, w] = acc[w].reshape(nplane, 2, per_dev, HEAD_DIM).astype(BF16)
                own[:, h, w] = acc[w, mine].reshape(2, per_dev, HEAD_DIM)

            def send_term(k, _):
                dst = to_earlier(k)
                term_copy(h, dst, plane).start()
                return 0

            lax.fori_loop(1, earlier, send_term, 0)

        return 0

    lax.fori_loop(0, heads * 2, step, 0)

    send_cross(heads + 1)
    send_cross(heads + 2)
    for h in range(heads):
        add_terms(h)

    part = per_dev // nhead
    half = heads // 2

    def sums_of(which, w):
        factor = scale if w == 0 else 1.0
        return [own[which, h, w] * factor for h in range(heads)]

    def share_of(blocks, dst):
        rows_of = slice(dst * part, (dst + 1) * part)
        pieces = [
            jnp.concatenate([blocks[w][b * half + a][rows_of] for a in range(half)], axis=1)
            for w in range(2)
            for b in range(2)
        ]
        return (jnp.concatenate(pieces, axis=0) * (1.0 / SPAN)).astype(BF16)

    mine = [sums_of(side, w) for w in range(2)]
    theirs = [sums_of(1 - side, w) for w in range(2)]
    for w in range(2):
        for h in range(heads):
            other_own[0, h, w] = theirs[w][h].astype(BF16)
    partial = pltpu.make_async_remote_copy(
        src_ref=other_own.at[0],
        dst_ref=other_own.at[1],
        send_sem=psend,
        recv_sem=precv,
        device_id={"seq": partner},
        device_id_type=MESH,
    )
    partial.start()
    for dst in range(nhead):
        sgs[0, dst] = share_of(mine, dst)
        sgs[1, dst] = share_of(theirs, dst)

    def shared_copy(at, shard, from_side, src, dst):
        return pltpu.make_async_remote_copy(
            src_ref=sgs.at[at, dst],
            dst_ref=shared.at[from_side, src],
            send_sem=ssend.at[at, dst],
            recv_sem=srecv.at[from_side, src],
            device_id={"seq": shard, "head": dst},
            device_id_type=MESH,
        )

    for k in range(1, nhead):
        other = lax.rem(hd + k, nhead)
        shared_copy(1, partner, side, hd, other).start()
        shared_copy(0, me, side, hd, other).start()
    for m in range(heads + 3, 2 * heads):
        send_cross(m)
    keep = pltpu.make_async_copy(sgs.at[0, hd], shared.at[side, hd], own_sem)
    keep.start()
    keep.wait()
    partial.wait()
    arrived = [[other_own[1, h, w].astype(F32) for h in range(heads)] for w in range(2)]
    gk_out[...] = jnp.concatenate([mine[0][h] + arrived[0][h] for h in range(heads)], axis=1)
    gv_out[...] = jnp.concatenate([mine[1][h] + arrived[1][h] for h in range(heads)], axis=1)
    for dst in range(nhead):

        @pl.when(hd == dst)
        def _():
            shared[1 - side, dst] = share_of(arrived, dst)

    for k in range(1, nhead):
        other = lax.rem(hd + k, nhead)
        for at, shard in ((1, partner), (0, me)):
            shared_copy(at, shard, side, hd, other).wait_send()
        for from_side in range(2):
            shared_copy(0, me, from_side, other, other).wait_recv()
        pltpu.make_async_remote_copy(
            src_ref=out.at[pl.ds(other * heads, heads)],
            dst_ref=out.at[pl.ds(other * heads, heads)],
            send_sem=asend.at[0, 0],
            recv_sem=arecv.at[other],
            device_id={"head": other},
            device_id_type=MESH,
        ).wait_recv()

    for copy in early:
        copy.wait_send()
    for m in range(heads - 1, 2 * heads):
        wait_cross(m)
    for c in range(2):
        pltpu.make_async_remote_copy(
            src_ref=tri.at[c],
            dst_ref=tri.at[c],
            send_sem=tsend.at[0],
            recv_sem=trecv.at[c],
            device_id={"head": other_chip},
            device_id_type=MESH,
        ).wait_recv()
    for h in range(heads):
        tile_copy(h, hd + 1 - 2 * lax.rem(hd, 2)).wait_send()
    for h in range(heads):
        pltpu.make_async_copy(stage.at[h, hd], out.at[hd * heads + h], local_sem.at[h]).wait()

    for w in range(2):
        swap_copy(w, side).wait_send()
    for h in range(heads):
        for kind in range(4):
            gather_each(kind, h, "sent")

        def term_sent(k, _, h=h):
            term_copy(h, to_earlier(k), plane).wait_send()
            return 0

        lax.fori_loop(1, earlier, term_sent, 0)


def finish_kernel(
    part, pieces, shared_ref, tri, gk_in, gv_in, q_out, k_out, v_out, gk_out, gv_out, kv, q_buf, k_buf, v_buf, load_sem, sem
):
    heads = pieces.shape[0]
    cols = 2 * shared_ref.shape[3]
    group = cols // HEAD_DIM
    loads = [
        pltpu.make_async_copy(pieces.at[h, 1:], kv.at[h], load_sem.at[0, h]) for h in range(heads)
    ]
    q_loads = [
        pltpu.make_async_copy(
            pieces.at[h, 0], q_buf.at[:, pl.ds(h * HEAD_DIM, HEAD_DIM)], load_sem.at[1, h]
        )
        for h in range(heads)
    ]
    copies = [
        pltpu.make_async_copy(gk_in, gk_out, sem.at[0]),
        pltpu.make_async_copy(gv_in, gv_out, sem.at[1]),
    ]
    for q_load, load in zip(q_loads, loads):
        q_load.start()
        load.start()
    for copy in copies:
        copy.start()
    chip = lax.axis_index("head") // 2
    lane = lax.broadcasted_iota(jnp.int32, (SPAN, 2 * SPAN), 1)
    low = lane < SPAN
    t_id = lax.rem(lane, SPAN)
    u_id = lax.broadcasted_iota(jnp.int32, (SPAN, 2 * SPAN), 0)
    shares = [
        shared_ref[0, g].astype(F32) + shared_ref[1, g].astype(F32) for g in range(heads // group)
    ]
    for g in range(heads // group):
        for b in range(group):
            h = g * group + b
            q_loads[h].wait()
            loads[h].wait()
            cols_of = slice(h * HEAD_DIM, (h + 1) * HEAD_DIM)

            def share(w, c, b=b, g=g):
                at = (2 * w + b // 2) * part + c
                sl = slice((b % 2) * HEAD_DIM, (b % 2 + 1) * HEAD_DIM)
                return shares[g][at : at + 1, sl]

            def as_sent(h=h, cols_of=cols_of, share=share):
                for w, buf in ((0, k_buf), (1, v_buf)):
                    for c in range(part):
                        rows = slice(c * SPAN, (c + 1) * SPAN)
                        buf[rows, cols_of] = (kv[h, w, rows].astype(F32) + share(w, c)).astype(BF16)

            def multiply(h=h, g=g, e=b - (group - EARLY), cols_of=cols_of, share=share):
                for p in range(part // 2):
                    rows = slice(p * 2 * SPAN, (p + 1) * 2 * SPAN)
                    block = tri[g % 2, e, :SPAN, rows].astype(F32)
                    main = tri[g % 2, e, SPAN : SPAN + 1, rows].astype(F32)
                    upper = jnp.where(u_id <= t_id, block, 0.0)
                    lower = jnp.where(u_id > t_id, block, jnp.where(u_id == t_id, main, 0.0))
                    for w, buf, x, dims, factor in (
                        (0, k_buf, upper, NN, HEAD_DIM ** (-0.5)),
                        (1, v_buf, lower, TN, 1.0),
                    ):
                        wide = jnp.concatenate(
                            [jnp.where(low, x, 0.0), jnp.where(low, 0.0, x)], axis=0
                        ).astype(BF16)
                        grad = dot(wide, kv[h, w, rows], dims) * factor
                        for c in range(2):
                            at = slice((2 * p + c) * SPAN, (2 * p + c + 1) * SPAN)
                            buf[at, cols_of] = (
                                grad[c * SPAN : (c + 1) * SPAN] + share(w, 2 * p + c)
                            ).astype(BF16)

            if b < group - EARLY:
                as_sent()
            else:
                pl.when(chip == g // 2)(as_sent)
                pl.when(chip != g // 2)(multiply)
        sl = pl.ds(g * cols, cols)
        for w, (buf, ref) in enumerate(((q_buf, q_out), (k_buf, k_out), (v_buf, v_out))):
            copy = pltpu.make_async_copy(
                buf.at[:, sl], ref.at[:, sl], sem.at[2 + 3 * g + w]
            )
            copy.start()
            copies.append(copy)
    for copy in copies:
        copy.wait()


def per_device(queries, keys, values, out_grad):
    count, cols = queries.shape
    nseq = lax.axis_size("seq")
    nhead = lax.axis_size("head")
    heads = cols // HEAD_DIM
    per_dev = count // SPAN
    total = per_dev * nseq
    tile = count // nhead
    part = per_dev // nhead
    nplane = nseq // 2
    anyspace = pl.BlockSpec(memory_space=pl.ANY)
    hbm = pl.BlockSpec(memory_space=pltpu.HBM)
    vmem = pl.BlockSpec(memory_space=pltpu.VMEM)
    dma = pltpu.SemaphoreType.DMA
    pieces, grad_k, grad_v, shared, tri = pl.pallas_call(
        functools.partial(main_kernel, nseq, nhead),
        out_shape=(
            jax.ShapeDtypeStruct((nhead * heads, 3, tile, HEAD_DIM), BF16),
            jax.ShapeDtypeStruct((per_dev, cols), F32),
            jax.ShapeDtypeStruct((per_dev, cols), F32),
            jax.ShapeDtypeStruct((2, nhead, 4 * part, cols // 2), BF16),
            jax.ShapeDtypeStruct((2, EARLY, SPAN + 16, tile), BF16),
        ),
        in_specs=[hbm] * 4,
        out_specs=(anyspace, vmem, vmem, vmem, vmem),
        scratch_shapes=[pltpu.VMEM((count, cols), BF16)] * 4
        + [
            pltpu.VMEM((heads, nplane // PLACES, PLACES, 2, per_dev, HEAD_DIM), BF16),
            pltpu.VMEM((heads, PLACES, nplane // PLACES, 2, per_dev, HEAD_DIM), BF16),
            pltpu.VMEM((HEAD_DIM, total), BF16),
            pltpu.VMEM((2, total, HEAD_DIM), F32),
            pltpu.VMEM((nplane, heads, 2, 2, per_dev, HEAD_DIM), BF16),
            pltpu.VMEM((nplane, heads, 2, 2, per_dev, HEAD_DIM), BF16),
            pltpu.VMEM((2, heads, 2, per_dev, HEAD_DIM), F32),
            pltpu.VMEM((2, heads, 2, per_dev, HEAD_DIM), BF16),
            pltpu.VMEM((2, nhead, 4 * part, cols // 2), BF16),
            pltpu.VMEM((heads, nhead, 3, tile, HEAD_DIM), BF16),
            pltpu.VMEM((EARLY + 1, 2, SPAN + 16, tile), BF16),
            pltpu.VMEM((2, total, tile), F32),
            pltpu.VMEM((2, total, tile), F32),
            dma((4, nhead)),
            dma((2,)),
            dma((2,)),
            dma((4, heads, PLACES)),
            dma((4, heads, PLACES)),
            dma((heads, nplane)),
            dma((heads, nplane)),
            dma,
            dma,
            dma((heads, nhead)),
            dma((nhead,)),
            dma((heads,)),
            dma((2, nhead)),
            dma((2, nhead)),
            dma,
            dma((EARLY, 2, 2)),
            dma((2 * EARLY,)),
            dma((2,)),
        ],
        compiler_params=pltpu.CompilerParams(
            collective_id=0, has_side_effects=True, vmem_limit_bytes=53 * 1024 * 1024
        ),
        name="attend",
    )(queries, keys, values, out_grad)
    row = jax.ShapeDtypeStruct((tile, nhead * cols), BF16)
    block = jax.ShapeDtypeStruct((per_dev, cols), F32)
    query_grad, key_grad, value_grad, grad_k, grad_v = pl.pallas_call(
        functools.partial(finish_kernel, part),
        out_shape=(row, row, row, block, block),
        in_specs=[hbm, vmem, vmem, vmem, vmem],
        out_specs=(hbm,) * 5,
        scratch_shapes=[
            pltpu.VMEM((nhead * heads, 2, tile, HEAD_DIM), BF16),
            pltpu.VMEM((tile, nhead * cols), BF16),
            pltpu.VMEM((tile, nhead * cols), BF16),
            pltpu.VMEM((tile, nhead * cols), BF16),
            dma((2, nhead * heads)),
            dma((2 + 3 * nhead,)),
        ],
        compiler_params=pltpu.CompilerParams(vmem_limit_bytes=53 * 1024 * 1024),
        name="finish",
    )(pieces, shared, tri, grad_k, grad_v)
    return (query_grad, key_grad, value_grad, grad_k, grad_v)


def solution(mesh):
    placed = (P("seq", "head"), P("seq", "head"), P("seq", "head"), P("seq", "head"))
    return jax.shard_map(
        per_device,
        mesh=mesh,
        in_specs=placed,
        out_specs=(
            P(("seq", "head"), None),
            P(("seq", "head"), None),
            P(("seq", "head"), None),
            P("seq", "head"),
            P("seq", "head"),
        ),
        check_vma=False,
    )
```

time: 60.4 us -> 57.4 us (0.950)
  Pallas kernels: 59.6 us -> 56.6 us
    pallas_call x1, Pallas kernels: 56.3 us -> 52.8 us  [per_device(): pl.pallas_call(functools.partial(main_kernel, nseq, nhead), out_shape=(ja...]
where the time goes in v4:
time: 57.4 us; the launch traced here: 57.3 us
  Pallas kernels  56.6 us (99%)
  between operations  0.64 us (1%)
    pallas_call x1, Pallas kernels, per_device(): pl.pallas_call(functools.partial(main_kernel, nseq, nhead), out_shape=(ja...  52.8 us
    pallas_call x1, Pallas kernels, per_device(): pl.pallas_call(functools.partial(finish_kernel, part), out_shape=(row, ro...  3.87 us

profile of v4, /device:TPU:1, one launch (start us, length us, event | category | flops | bytes accessed | tf_op | source)
XLA Modules:
  0.0 57.3 jit_solution(16419739653792177606)
XLA Ops:
  0.6 52.8 %attend.1 = (bf16[16,3,256,128]{3,2,1,0:T(8,128)(2,1)}, f32[16,512]{1,0:T(8,128)S(1)}, f32[16,512]{1,0:T(8,128)S(1)}, bf16[2,4,16,256]{3,2,1,0:T(8,128)(2,1)S(1)}, bf16[2,2,80,256]{3,2,1,0:T(8,128)(2,1)S(1)}) custom-call(bf16[1024,512]{1,0:T(8,128)(2,1)} %q_hbm.1, bf16[1024,512]{1,0:T(8,128)(2,1)} %k_hbm.1, bf16[1024,512]{1,0:T(8,128)(2,1)} %v_hbm.1, ...), custom_call_target="tpu_custom_call" | custom-call | tf_op jit(solution)/shard_map/attend/pallas_call | solution.py:666
  53.4 3.9 %finish.1 = (bf16[256,2048]{1,0:T(8,128)(2,1)}, bf16[256,2048]{1,0:T(8,128)(2,1)}, bf16[256,2048]{1,0:T(8,128)(2,1)}, f32[16,512]{1,0:T(8,128)}, f32[16,512]{1,0:T(8,128)}) custom-call(bf16[16,3,256,128]{3,2,1,0:T(8,128)(2,1)} %get-tuple-element.10.pieces, bf16[2,4,16,256]{3,2,1,0:T(8,128)(2,1)S(1)} %get-tuple-element.11.shared_ref, ...), custom_call_target="tpu_custom_call" | custom-call | tf_op jit(solution)/shard_map/finish/pallas_call | solution.py:718

commit v5 on v4

--- a/solution.py
+++ b/solution.py
@@ -85,6 +85,17 @@
 
     lax.fori_loop(1, nplane, greet, 0)
     pl.semaphore_signal(barrier, inc=1, device_id={"seq": partner}, device_id_type=MESH)
+    for k in range(1, PLACES):
+        for p in (
+            slab * PLACES + lax.rem(place + k, PLACES),
+            lax.rem(slab + k, PLACES) * PLACES + place,
+        ):
+            pl.semaphore_signal(
+                barrier,
+                inc=1,
+                device_id={"seq": shard_at(p) + partner - me},
+                device_id_type=MESH,
+            )
     for i in range(1, nhead):
         for shard in (me, partner):
             pl.semaphore_signal(
@@ -109,12 +120,12 @@
             else:
                 sumv[h, place, slab, side] = block
 
-    pl.semaphore_wait(barrier, nplane - 1 + 1 + 2 * (nhead - 1))
+    pl.semaphore_wait(barrier, nplane - 1 + 1 + 2 * (PLACES - 1) + 2 * (nhead - 1))
 
     slabs = nplane // PLACES
 
     def swap_copy(w, to):
-        ref = sumk.at[:, slab, place, to] if w == 0 else sumv.at[:, place, slab, to]
+        ref = sumk.at[1:, slab, place, to] if w == 0 else sumv.at[1:, place, slab, to]
         return pltpu.make_async_remote_copy(
             src_ref=ref,
             dst_ref=ref,
@@ -173,6 +184,33 @@
     def to_earlier(k):
         return lax.rem(plane + k, earlier)
 
+    def direct_copy(w, of, dst, across):
+        ref = sumk.at[0, slab, place, of] if w == 0 else sumv.at[0, place, slab, of]
+        p = slab * PLACES + dst if w == 0 else dst * PLACES + place
+        return pltpu.make_async_remote_copy(
+            src_ref=ref,
+            dst_ref=ref,
+            send_sem=gsend.at[w, 0, dst],
+            recv_sem=grecv.at[w, 0, place if w == 0 else slab],
+            device_id={"seq": shard_at(p) + across * (partner - me)},
+            device_id_type=MESH,
+        )
+
+    for k in range(PLACES):
+        for across in (1, 0):
+            if k > 0 or across:
+                direct_copy(0, side, lax.rem(place + k, PLACES), across).start()
+
+    def direct_values(dst, _):
+        direct_copy(1, side, dst, 1).start()
+
+        @pl.when(dst > slab)
+        def _():
+            direct_copy(1, side, dst, 0).start()
+
+        return 0
+
+    lax.fori_loop(slab, slabs, direct_values, 0)
     for w in range(2):
         swap_copy(w, side).start()
     for group in loads[2:]:
@@ -182,6 +220,9 @@
     plain = heads - EARLY
 
     other_chip = (1 - hd // 2) * 2
+
+    def goes_early(e, j):
+        return e < EARLY - 1 or j == 0
 
     def early_copy(e, j, w):
         ref = (q_ref, d_ref)[w]
@@ -196,15 +237,19 @@
             device_id_type=MESH,
         )
 
-    early = [early_copy(e, j, w) for e in range(EARLY) for j in range(2) for w in range(2)]
+    early = [early_copy(e, j, w) for e in range(EARLY) for j in range(2) for w in range(2) if goes_early(e, j)]
     for copy in early:
         copy.start()
+    for kind in (0, 1):
+        direct_copy(kind, 1 - side, place if kind == 0 else slab, 1).wait_recv()
+        gather_each(kind, 0, "arrived")
+        gather_each(kind + 2, 0, "start")
     for w in range(2):
         swap_copy(w, 1 - side).wait_recv()
-    for h in range(heads):
+    for h in range(1, heads):
         for kind in (0, 1):
             gather_each(kind, h, "start")
-    for h in range(heads):
+    for h in range(1, heads):
         for kind in (0, 1):
             gather_each(kind, h, "arrived")
             gather_each(kind + 2, h, "start")
@@ -278,7 +323,7 @@
     def send_cross(m):
         for packed in (False, True):
 
-            @pl.when((m >= 2 * plain) == packed)
+            @pl.when(((m >= 2 * plain) & (m < 2 * heads - 1)) == packed)
             def _():
                 for copy in cross_copies(m, packed):
                     copy.start()
@@ -286,7 +331,7 @@
     def wait_cross(m):
         for packed in (False, True):
 
-            @pl.when((m >= 2 * plain) == packed)
+            @pl.when(((m >= 2 * plain) & (m < 2 * heads - 1)) == packed)
             def _():
                 for copy in cross_copies(m, packed):
                     copy.wait_send()
@@ -536,14 +581,19 @@
     for m in range(heads - 1, 2 * heads):
         wait_cross(m)
     for c in range(2):
-        pltpu.make_async_remote_copy(
-            src_ref=tri.at[c],
-            dst_ref=tri.at[c],
-            send_sem=tsend.at[0],
-            recv_sem=trecv.at[c],
-            device_id={"head": other_chip},
-            device_id_type=MESH,
-        ).wait_recv()
+        for core, blocks in ((0, EARLY), (1, EARLY - 1)):
+
+            @pl.when(lax.rem(hd, 2) == core)
+            def _():
+                pltpu.make_async_remote_copy(
+                    src_ref=tri.at[c, :blocks],
+                    dst_ref=tri.at[c, :blocks],
+                    send_sem=tsend.at[0],
+                    recv_sem=trecv.at[c],
+                    device_id={"head": other_chip},
+                    device_id_type=MESH,
+                ).wait_recv()
+
     for h in range(heads):
         tile_copy(h, hd + 1 - 2 * lax.rem(hd, 2)).wait_send()
     for h in range(heads):
@@ -551,6 +601,7 @@
 
     for w in range(2):
         swap_copy(w, side).wait_send()
+        direct_copy(w, side, place if w == 0 else slab, 1).wait_send()
     for h in range(heads):
         for kind in range(4):
             gather_each(kind, h, "sent")
@@ -569,24 +620,21 @@
     cols = 2 * shared_ref.shape[3]
     group = cols // HEAD_DIM
     loads = [
-        pltpu.make_async_copy(pieces.at[h, 1:], kv.at[h], load_sem.at[0, h]) for h in range(heads)
-    ]
-    q_loads = [
         pltpu.make_async_copy(
-            pieces.at[h, 0], q_buf.at[:, pl.ds(h * HEAD_DIM, HEAD_DIM)], load_sem.at[1, h]
-        )
-        for h in range(heads)
+            pieces.at[g * group : (g + 1) * group], kv.at[g * group : (g + 1) * group], load_sem.at[g]
+        )
+        for g in range(heads // group)
     ]
     copies = [
         pltpu.make_async_copy(gk_in, gk_out, sem.at[0]),
         pltpu.make_async_copy(gv_in, gv_out, sem.at[1]),
     ]
-    for q_load, load in zip(q_loads, loads):
-        q_load.start()
+    for load in loads:
         load.start()
     for copy in copies:
         copy.start()
     chip = lax.axis_index("head") // 2
+    core = lax.rem(lax.axis_index("head"), 2)
     lane = lax.broadcasted_iota(jnp.int32, (SPAN, 2 * SPAN), 1)
     low = lane < SPAN
     t_id = lax.rem(lane, SPAN)
@@ -595,11 +643,11 @@
         shared_ref[0, g].astype(F32) + shared_ref[1, g].astype(F32) for g in range(heads // group)
     ]
     for g in range(heads // group):
+        loads[g].wait()
         for b in range(group):
             h = g * group + b
-            q_loads[h].wait()
-            loads[h].wait()
             cols_of = slice(h * HEAD_DIM, (h + 1) * HEAD_DIM)
+            q_buf[:, cols_of] = kv[h, 0]
 
             def share(w, c, b=b, g=g):
                 at = (2 * w + b // 2) * part + c
@@ -610,7 +658,7 @@
                 for w, buf in ((0, k_buf), (1, v_buf)):
                     for c in range(part):
                         rows = slice(c * SPAN, (c + 1) * SPAN)
-                        buf[rows, cols_of] = (kv[h, w, rows].astype(F32) + share(w, c)).astype(BF16)
+                        buf[rows, cols_of] = (kv[h, 1 + w, rows].astype(F32) + share(w, c)).astype(BF16)
 
             def multiply(h=h, g=g, e=b - (group - EARLY), cols_of=cols_of, share=share):
                 for p in range(part // 2):
@@ -626,7 +674,7 @@
                         wide = jnp.concatenate(
                             [jnp.where(low, x, 0.0), jnp.where(low, 0.0, x)], axis=0
                         ).astype(BF16)
-                        grad = dot(wide, kv[h, w, rows], dims) * factor
+                        grad = dot(wide, kv[h, 1 + w, rows], dims) * factor
                         for c in range(2):
                             at = slice((2 * p + c) * SPAN, (2 * p + c + 1) * SPAN)
                             buf[at, cols_of] = (
@@ -636,8 +684,11 @@
             if b < group - EARLY:
                 as_sent()
             else:
-                pl.when(chip == g // 2)(as_sent)
-                pl.when(chip != g // 2)(multiply)
+                packed = chip != g // 2
+                if b == group - 1:
+                    packed = packed & (core == 0)
+                pl.when(jnp.logical_not(packed))(as_sent)
+                pl.when(packed)(multiply)
         sl = pl.ds(g * cols, cols)
         for w, (buf, ref) in enumerate(((q_buf, q_out), (k_buf, k_out), (v_buf, v_out))):
             copy = pltpu.make_async_copy(
@@ -721,11 +772,11 @@
         in_specs=[hbm, vmem, vmem, vmem, vmem],
         out_specs=(hbm,) * 5,
         scratch_shapes=[
-            pltpu.VMEM((nhead * heads, 2, tile, HEAD_DIM), BF16),
+            pltpu.VMEM((nhead * heads, 3, tile, HEAD_DIM), BF16),
             pltpu.VMEM((tile, nhead * cols), BF16),
             pltpu.VMEM((tile, nhead * cols), BF16),
             pltpu.VMEM((tile, nhead * cols), BF16),
-            dma((2, nhead * heads)),
+            dma((nhead,)),
             dma((2 + 3 * nhead,)),
         ],
         compiler_params=pltpu.CompilerParams(vmem_limit_bytes=53 * 1024 * 1024),

time: 57.4 us -> 56.3 us (0.981)
  Pallas kernels: 56.6 us -> 55.5 us
    pallas_call x1, Pallas kernels: 52.8 us -> 52.1 us  [per_device(): pl.pallas_call(functools.partial(main_kernel, nseq, nhead), out_shape=(ja...]
where the time goes in v5:
time: 56.3 us; the launch traced here: 56.2 us
  Pallas kernels  55.5 us (99%)
  between operations  0.64 us (1%)
    pallas_call x1, Pallas kernels, per_device(): pl.pallas_call(functools.partial(main_kernel, nseq, nhead), out_shape=(ja...  52.1 us
    pallas_call x1, Pallas kernels, per_device(): pl.pallas_call(functools.partial(finish_kernel, part), out_shape=(row, ro...  3.43 us

profile of v5, /device:TPU:1, one launch (start us, length us, event | category | flops | bytes accessed | tf_op | source)
XLA Modules:
  0.0 56.2 jit_solution(1153030154929344703)
XLA Ops:
  0.6 52.1 %attend.1 = (bf16[16,3,256,128]{3,2,1,0:T(8,128)(2,1)}, f32[16,512]{1,0:T(8,128)S(1)}, f32[16,512]{1,0:T(8,128)S(1)}, bf16[2,4,16,256]{3,2,1,0:T(8,128)(2,1)S(1)}, bf16[2,2,80,256]{3,2,1,0:T(8,128)(2,1)S(1)}) custom-call(bf16[1024,512]{1,0:T(8,128)(2,1)} %q_hbm.1, bf16[1024,512]{1,0:T(8,128)(2,1)} %k_hbm.1, bf16[1024,512]{1,0:T(8,128)(2,1)} %v_hbm.1, ...), custom_call_target="tpu_custom_call" | custom-call | tf_op jit(solution)/shard_map/attend/pallas_call | solution.py:717
  52.7 3.4 %finish.1 = (bf16[256,2048]{1,0:T(8,128)(2,1)}, bf16[256,2048]{1,0:T(8,128)(2,1)}, bf16[256,2048]{1,0:T(8,128)(2,1)}, f32[16,512]{1,0:T(8,128)}, f32[16,512]{1,0:T(8,128)}) custom-call(bf16[16,3,256,128]{3,2,1,0:T(8,128)(2,1)} %get-tuple-element.10.pieces, bf16[2,4,16,256]{3,2,1,0:T(8,128)(2,1)S(1)} %get-tuple-element.11.shared_ref, ...), custom_call_target="tpu_custom_call" | custom-call | tf_op jit(solution)/shard_map/finish/pallas_call | solution.py:769

commit v6 on v5

--- a/solution.py
+++ b/solution.py
@@ -614,23 +614,15 @@
 
 
 def finish_kernel(
-    part, pieces, shared_ref, tri, gk_in, gv_in, q_out, k_out, v_out, gk_out, gv_out, kv, q_buf, k_buf, v_buf, load_sem, sem
+    part, pieces, shared_ref, tri, gk_in, gv_in, q_out, k_out, v_out, gk_out, gv_out, q_buf, k_buf, v_buf, sem
 ):
     heads = pieces.shape[0]
     cols = 2 * shared_ref.shape[3]
     group = cols // HEAD_DIM
-    loads = [
-        pltpu.make_async_copy(
-            pieces.at[g * group : (g + 1) * group], kv.at[g * group : (g + 1) * group], load_sem.at[g]
-        )
-        for g in range(heads // group)
-    ]
     copies = [
         pltpu.make_async_copy(gk_in, gk_out, sem.at[0]),
         pltpu.make_async_copy(gv_in, gv_out, sem.at[1]),
     ]
-    for load in loads:
-        load.start()
     for copy in copies:
         copy.start()
     chip = lax.axis_index("head") // 2
@@ -643,11 +635,10 @@
         shared_ref[0, g].astype(F32) + shared_ref[1, g].astype(F32) for g in range(heads // group)
     ]
     for g in range(heads // group):
-        loads[g].wait()
         for b in range(group):
             h = g * group + b
             cols_of = slice(h * HEAD_DIM, (h + 1) * HEAD_DIM)
-            q_buf[:, cols_of] = kv[h, 0]
+            q_buf[:, cols_of] = pieces[h, 0]
 
             def share(w, c, b=b, g=g):
                 at = (2 * w + b // 2) * part + c
@@ -658,7 +649,7 @@
                 for w, buf in ((0, k_buf), (1, v_buf)):
                     for c in range(part):
                         rows = slice(c * SPAN, (c + 1) * SPAN)
-                        buf[rows, cols_of] = (kv[h, 1 + w, rows].astype(F32) + share(w, c)).astype(BF16)
+                        buf[rows, cols_of] = (pieces[h, 1 + w, rows].astype(F32) + share(w, c)).astype(BF16)
 
             def multiply(h=h, g=g, e=b - (group - EARLY), cols_of=cols_of, share=share):
                 for p in range(part // 2):
@@ -674,7 +665,7 @@
                         wide = jnp.concatenate(
                             [jnp.where(low, x, 0.0), jnp.where(low, 0.0, x)], axis=0
                         ).astype(BF16)
-                        grad = dot(wide, kv[h, 1 + w, rows], dims) * factor
+                        grad = dot(wide, pieces[h, 1 + w, rows], dims) * factor
                         for c in range(2):
                             at = slice((2 * p + c) * SPAN, (2 * p + c + 1) * SPAN)
                             buf[at, cols_of] = (
@@ -717,14 +708,14 @@
     pieces, grad_k, grad_v, shared, tri = pl.pallas_call(
         functools.partial(main_kernel, nseq, nhead),
         out_shape=(
-            jax.ShapeDtypeStruct((nhead * heads, 3, tile, HEAD_DIM), BF16),
+            pltpu.VMEM((nhead * heads, 3, tile, HEAD_DIM), BF16),
             jax.ShapeDtypeStruct((per_dev, cols), F32),
             jax.ShapeDtypeStruct((per_dev, cols), F32),
             jax.ShapeDtypeStruct((2, nhead, 4 * part, cols // 2), BF16),
             jax.ShapeDtypeStruct((2, EARLY, SPAN + 16, tile), BF16),
         ),
         in_specs=[hbm] * 4,
-        out_specs=(anyspace, vmem, vmem, vmem, vmem),
+        out_specs=(vmem, vmem, vmem, vmem, vmem),
         scratch_shapes=[pltpu.VMEM((count, cols), BF16)] * 4
         + [
             pltpu.VMEM((heads, nplane // PLACES, PLACES, 2, per_dev, HEAD_DIM), BF16),
@@ -760,7 +751,7 @@
             dma((2,)),
         ],
         compiler_params=pltpu.CompilerParams(
-            collective_id=0, has_side_effects=True, vmem_limit_bytes=53 * 1024 * 1024
+            collective_id=0, has_side_effects=True, vmem_limit_bytes=50 * 1024 * 1024
         ),
         name="attend",
     )(queries, keys, values, out_grad)
@@ -769,17 +760,15 @@
     query_grad, key_grad, value_grad, grad_k, grad_v = pl.pallas_call(
         functools.partial(finish_kernel, part),
         out_shape=(row, row, row, block, block),
-        in_specs=[hbm, vmem, vmem, vmem, vmem],
+        in_specs=[vmem, vmem, vmem, vmem, vmem],
         out_specs=(hbm,) * 5,
         scratch_shapes=[
-            pltpu.VMEM((nhead * heads, 3, tile, HEAD_DIM), BF16),
             pltpu.VMEM((tile, nhead * cols), BF16),
             pltpu.VMEM((tile, nhead * cols), BF16),
             pltpu.VMEM((tile, nhead * cols), BF16),
-            dma((nhead,)),
             dma((2 + 3 * nhead,)),
         ],
-        compiler_params=pltpu.CompilerParams(vmem_limit_bytes=53 * 1024 * 1024),
+        compiler_params=pltpu.CompilerParams(vmem_limit_bytes=50 * 1024 * 1024),
         name="finish",
     )(pieces, shared, tri, grad_k, grad_v)
     return (query_grad, key_grad, value_grad, grad_k, grad_v)

time: 56.3 us -> 54.9 us (0.975)
  Pallas kernels: 55.5 us -> 54.2 us
    pallas_call x1, Pallas kernels: 3.43 us -> 2.19 us  [per_device(): pl.pallas_call(functools.partial(finish_kernel, part), out_shape=(row, ro...]
where the time goes in v6:
time: 54.9 us; the launch traced here: 54.8 us
  Pallas kernels  54.2 us (99%)
  between operations  0.64 us (1%)
    pallas_call x1, Pallas kernels, per_device(): pl.pallas_call(functools.partial(main_kernel, nseq, nhead), out_shape=(pl...  52 us
    pallas_call x1, Pallas kernels, per_device(): pl.pallas_call(functools.partial(finish_kernel, part), out_shape=(row, ro...  2.19 us

profile of v6, /device:TPU:1, one launch (start us, length us, event | category | flops | bytes accessed | tf_op | source)
XLA Modules:
  0.0 54.8 jit_solution(4434150366231738935)
XLA Ops:
  0.6 52.0 %attend.1 = (bf16[16,3,256,128]{3,2,1,0:T(8,128)(2,1)S(1)}, f32[16,512]{1,0:T(8,128)S(1)}, f32[16,512]{1,0:T(8,128)S(1)}, bf16[2,4,16,256]{3,2,1,0:T(8,128)(2,1)S(1)}, bf16[2,2,80,256]{3,2,1,0:T(8,128)(2,1)S(1)}) custom-call(bf16[1024,512]{1,0:T(8,128)(2,1)} %q_hbm.1, bf16[1024,512]{1,0:T(8,128)(2,1)} %k_hbm.1, bf16[1024,512]{1,0:T(8,128)(2,1)} %v_hbm.1, ...), custom_call_target="tpu_custom_call" | custom-call | tf_op jit(solution)/shard_map/attend/pallas_call | solution.py:708
  52.6 2.2 %finish.1 = (bf16[256,2048]{1,0:T(8,128)(2,1)}, bf16[256,2048]{1,0:T(8,128)(2,1)}, bf16[256,2048]{1,0:T(8,128)(2,1)}, f32[16,512]{1,0:T(8,128)}, f32[16,512]{1,0:T(8,128)}) custom-call(bf16[16,3,256,128]{3,2,1,0:T(8,128)(2,1)S(1)} %get-tuple-element.10.pieces, bf16[2,4,16,256]{3,2,1,0:T(8,128)(2,1)S(1)} %get-tuple-element.11.shared_ref, ...), custom_call_target="tpu_custom_call" | custom-call | tf_op jit(solution)/shard_map/finish/pallas_call | solution.py:760

commit v7 on v6

--- a/solution.py
+++ b/solution.py
@@ -614,7 +614,7 @@
 
 
 def finish_kernel(
-    part, pieces, shared_ref, tri, gk_in, gv_in, q_out, k_out, v_out, gk_out, gv_out, q_buf, k_buf, v_buf, sem
+    part, pieces, shared_ref, tri, gk_in, gv_in, q_out, k_out, v_out, gk_out, gv_out, k_buf, v_buf, sem
 ):
     heads = pieces.shape[0]
     cols = 2 * shared_ref.shape[3]
@@ -623,39 +623,46 @@
         pltpu.make_async_copy(gk_in, gk_out, sem.at[0]),
         pltpu.make_async_copy(gv_in, gv_out, sem.at[1]),
     ]
+    for h in range(heads):
+        copies.append(
+            pltpu.make_async_copy(
+                pieces.at[h, 0], q_out.at[:, pl.ds(h * HEAD_DIM, HEAD_DIM)], sem.at[2 + h]
+            )
+        )
     for copy in copies:
         copy.start()
     chip = lax.axis_index("head") // 2
     core = lax.rem(lax.axis_index("head"), 2)
+    head_of = [lax.rem(2 * (1 - chip) + g, heads // group) for g in range(heads // group)]
     lane = lax.broadcasted_iota(jnp.int32, (SPAN, 2 * SPAN), 1)
     low = lane < SPAN
     t_id = lax.rem(lane, SPAN)
     u_id = lax.broadcasted_iota(jnp.int32, (SPAN, 2 * SPAN), 0)
     shares = [
-        shared_ref[0, g].astype(F32) + shared_ref[1, g].astype(F32) for g in range(heads // group)
+        shared_ref[0, g].astype(F32) + shared_ref[1, g].astype(F32) for g in head_of
     ]
     for g in range(heads // group):
         for b in range(group):
             h = g * group + b
+            slot = head_of[g] * group + b
             cols_of = slice(h * HEAD_DIM, (h + 1) * HEAD_DIM)
-            q_buf[:, cols_of] = pieces[h, 0]
 
             def share(w, c, b=b, g=g):
                 at = (2 * w + b // 2) * part + c
                 sl = slice((b % 2) * HEAD_DIM, (b % 2 + 1) * HEAD_DIM)
                 return shares[g][at : at + 1, sl]
 
-            def as_sent(h=h, cols_of=cols_of, share=share):
+            def as_sent(slot=slot, cols_of=cols_of, share=share):
                 for w, buf in ((0, k_buf), (1, v_buf)):
                     for c in range(part):
                         rows = slice(c * SPAN, (c + 1) * SPAN)
-                        buf[rows, cols_of] = (pieces[h, 1 + w, rows].astype(F32) + share(w, c)).astype(BF16)
-
-            def multiply(h=h, g=g, e=b - (group - EARLY), cols_of=cols_of, share=share):
+                        buf[rows, cols_of] = (pieces[slot, 1 + w, rows].astype(F32) + share(w, c)).astype(BF16)
+
+            def multiply(slot=slot, g=g, e=b - (group - EARLY), cols_of=cols_of, share=share):
                 for p in range(part // 2):
                     rows = slice(p * 2 * SPAN, (p + 1) * 2 * SPAN)
-                    block = tri[g % 2, e, :SPAN, rows].astype(F32)
-                    main = tri[g % 2, e, SPAN : SPAN + 1, rows].astype(F32)
+                    block = tri[g, e, :SPAN, rows].astype(F32)
+                    main = tri[g, e, SPAN : SPAN + 1, rows].astype(F32)
                     upper = jnp.where(u_id <= t_id, block, 0.0)
                     lower = jnp.where(u_id > t_id, block, jnp.where(u_id == t_id, main, 0.0))
                     for w, buf, x, dims, factor in (
@@ -665,25 +672,26 @@
                         wide = jnp.concatenate(
                             [jnp.where(low, x, 0.0), jnp.where(low, 0.0, x)], axis=0
                         ).astype(BF16)
-                        grad = dot(wide, pieces[h, 1 + w, rows], dims) * factor
+                        grad = dot(wide, pieces[slot, 1 + w, rows], dims) * factor
                         for c in range(2):
                             at = slice((2 * p + c) * SPAN, (2 * p + c + 1) * SPAN)
                             buf[at, cols_of] = (
                                 grad[c * SPAN : (c + 1) * SPAN] + share(w, 2 * p + c)
                             ).astype(BF16)
 
-            if b < group - EARLY:
+            if g > 1 or b < group - EARLY:
                 as_sent()
+            elif b < group - 1:
+                multiply()
             else:
-                packed = chip != g // 2
-                if b == group - 1:
-                    packed = packed & (core == 0)
-                pl.when(jnp.logical_not(packed))(as_sent)
-                pl.when(packed)(multiply)
+                pl.when(core != 0)(as_sent)
+                pl.when(core == 0)(multiply)
         sl = pl.ds(g * cols, cols)
-        for w, (buf, ref) in enumerate(((q_buf, q_out), (k_buf, k_out), (v_buf, v_out))):
+        for w, (buf, ref) in enumerate(((k_buf, k_out), (v_buf, v_out))):
             copy = pltpu.make_async_copy(
-                buf.at[:, sl], ref.at[:, sl], sem.at[2 + 3 * g + w]
+                buf.at[:, sl],
+                ref.at[:, pl.ds(pl.multiple_of(head_of[g] * cols, cols), cols)],
+                sem.at[2 + heads + 2 * g + w]
             )
             copy.start()
             copies.append(copy)
@@ -765,8 +773,7 @@
         scratch_shapes=[
             pltpu.VMEM((tile, nhead * cols), BF16),
             pltpu.VMEM((tile, nhead * cols), BF16),
-            pltpu.VMEM((tile, nhead * cols), BF16),
-            dma((2 + 3 * nhead,)),
+            dma((2 + nhead * heads + 2 * nhead,)),
         ],
         compiler_params=pltpu.CompilerParams(vmem_limit_bytes=50 * 1024 * 1024),
         name="finish",

time: 54.9 us -> 54.7 us (level)
  no operation moved by 1% of the time
where the time goes in v7:
time: 54.7 us; the launch traced here: 54.6 us
  Pallas kernels  53.9 us (99%)
  between operations  0.64 us (1%)
    pallas_call x1, Pallas kernels, per_device(): pl.pallas_call(functools.partial(main_kernel, nseq, nhead), out_shape=(pl...  52 us
    pallas_call x1, Pallas kernels, per_device(): pl.pallas_call(functools.partial(finish_kernel, part), out_shape=(row, ro...  1.94 us

profile of v7, /device:TPU:1, one launch (start us, length us, event | category | flops | bytes accessed | tf_op | source)
XLA Modules:
  0.0 54.6 jit_solution(11848100437361057238)
XLA Ops:
  0.6 52.0 %attend.1 = (bf16[16,3,256,128]{3,2,1,0:T(8,128)(2,1)S(1)}, f32[16,512]{1,0:T(8,128)S(1)}, f32[16,512]{1,0:T(8,128)S(1)}, bf16[2,4,16,256]{3,2,1,0:T(8,128)(2,1)S(1)}, bf16[2,2,80,256]{3,2,1,0:T(8,128)(2,1)S(1)}) custom-call(bf16[1024,512]{1,0:T(8,128)(2,1)} %q_hbm.1, bf16[1024,512]{1,0:T(8,128)(2,1)} %k_hbm.1, bf16[1024,512]{1,0:T(8,128)(2,1)} %v_hbm.1, ...), custom_call_target="tpu_custom_call" | custom-call | tf_op jit(solution)/shard_map/attend/pallas_call | solution.py:716
  52.6 1.9 %finish.1 = (bf16[256,2048]{1,0:T(8,128)(2,1)}, bf16[256,2048]{1,0:T(8,128)(2,1)}, bf16[256,2048]{1,0:T(8,128)(2,1)}, f32[16,512]{1,0:T(8,128)}, f32[16,512]{1,0:T(8,128)}) custom-call(bf16[16,3,256,128]{3,2,1,0:T(8,128)(2,1)S(1)} %get-tuple-element.10.pieces, bf16[2,4,16,256]{3,2,1,0:T(8,128)(2,1)S(1)} %get-tuple-element.11.shared_ref, ...), custom_call_target="tpu_custom_call" | custom-call | tf_op jit(solution)/shard_map/finish/pallas_call | solution.py:768

commit v8 on v7

--- a/solution.py
+++ b/solution.py
@@ -472,6 +472,10 @@
 
             send_cross(h + 1)
 
+            @pl.when(h >= 2)
+            def _():
+                add_terms(h - 2)
+
 
         @pl.when(own_chip == 1)
         def _():
@@ -495,7 +499,7 @@
 
     send_cross(heads + 1)
     send_cross(heads + 2)
-    for h in range(heads):
+    for h in range(heads - 2, heads):
         add_terms(h)
 
     part = per_dev // nhead

time: 54.7 us -> 54.7 us (level)
  no operation moved by 1% of the time
where the time goes in v8:
time: 54.7 us; the launch traced here: 54.6 us
  Pallas kernels  53.9 us (99%)
  between operations  0.64 us (1%)
    pallas_call x1, Pallas kernels, per_device(): pl.pallas_call(functools.partial(main_kernel, nseq, nhead), out_shape=(pl...  52 us
    pallas_call x1, Pallas kernels, per_device(): pl.pallas_call(functools.partial(finish_kernel, part), out_shape=(row, ro...  1.94 us

profile of v8, /device:TPU:1, one launch (start us, length us, event | category | flops | bytes accessed | tf_op | source)
XLA Modules:
  0.0 54.6 jit_solution(7779838135080323630)
XLA Ops:
  0.6 52.0 %attend.1 = (bf16[16,3,256,128]{3,2,1,0:T(8,128)(2,1)S(1)}, f32[16,512]{1,0:T(8,128)S(1)}, f32[16,512]{1,0:T(8,128)S(1)}, bf16[2,4,16,256]{3,2,1,0:T(8,128)(2,1)S(1)}, bf16[2,2,80,256]{3,2,1,0:T(8,128)(2,1)S(1)}) custom-call(bf16[1024,512]{1,0:T(8,128)(2,1)} %q_hbm.1, bf16[1024,512]{1,0:T(8,128)(2,1)} %k_hbm.1, bf16[1024,512]{1,0:T(8,128)(2,1)} %v_hbm.1, ...), custom_call_target="tpu_custom_call" | custom-call | tf_op jit(solution)/shard_map/attend/pallas_call | solution.py:720
  52.6 1.9 %finish.1 = (bf16[256,2048]{1,0:T(8,128)(2,1)}, bf16[256,2048]{1,0:T(8,128)(2,1)}, bf16[256,2048]{1,0:T(8,128)(2,1)}, f32[16,512]{1,0:T(8,128)}, f32[16,512]{1,0:T(8,128)}) custom-call(bf16[16,3,256,128]{3,2,1,0:T(8,128)(2,1)S(1)} %get-tuple-element.10.pieces, bf16[2,4,16,256]{3,2,1,0:T(8,128)(2,1)S(1)} %get-tuple-element.11.shared_ref, ...), custom_call_target="tpu_custom_call" | custom-call | tf_op jit(solution)/shard_map/finish/pallas_call | solution.py:772
